TPU v7x, 32 devices: a whole 2x2x4 slice. The times are simulated.
32 devices in a mesh: own: 4 (over z), col: 2 (over x), mlp: 4 (over y, core).
Axes of the slice: x: 2, y: 2, z: 4, core: 2. Of those that a mesh axis runs over, the one named last changes fastest.
Arguments:
- features: bfloat16 [32768, 512], P(('own', 'col')), may hold values from -6 to 6
- nbr_page: int32 [1024, 32], P(('own', 'col')), may hold values from 0 to 32767, as said below
- nbr_weight: bfloat16 [1024, 32], P(('own', 'col')), may hold values from 0.0049743652 to 0.29882812
- labels: int32 [1024], P(('own', 'col')), may hold values from 0 to 255
- w_one: bfloat16 [512, 2048], P(None, 'mlp'), may hold values from -0.25 to 0.25
- w_two: bfloat16 [2048, 256], P('mlp'), may hold values from -0.125 to 0.125
Outputs:
- grad_one: float32 [512, 2048], P(None, 'mlp')
- grad_two: float32 [2048, 256], P('mlp')
Inputs may be any that keep to these rules, and one draw needn't show every extreme that they name: `nbr_page`: page p is held by owner p // 4096 (owners numbered along own then col) at its row p % 4096. The 32 neighbours of a target are distinct pages listed in non-decreasing order of owner. Of the 4096 neighbour entries of the targets of one index of own and col, at most 1024 fall on one owner; one owner receives exactly 1024 entries from every index, and some owners receive none from some indices.
All inputs are finite; a program needn't handle non-finite values.
Results may differ from a plain program's by a relative error of at most 0.011.
Values may be sent and summed in bfloat16 or wider, within the bound.
A program may use at most 128 MiB of HBM per device.

v0:
```python
import jax
import jax.numpy as jnp
from jax import lax
from jax.sharding import PartitionSpec as P


def body(features, nbr_page, nbr_weight, labels, w_one, w_two):
    rows_dev = features.shape[0]
    width_f = features.shape[1]
    targets = nbr_page.shape[0]
    width_k = nbr_page.shape[1]
    owners = lax.axis_size(("own", "col"))
    entries = targets * width_k
    capacity = 2 * entries // owners
    owner_ids = nbr_page // rows_dev
    local_row = nbr_page % rows_dev
    owner_range = jnp.arange(owners, dtype=jnp.int32)
    matches = (owner_ids[:, :, None] == owner_range[None, None, :]).astype(jnp.int32)
    row_count = jnp.sum(matches, axis=1)
    earlier_rows = jnp.cumsum(row_count, axis=0) - row_count
    before_owner = jnp.cumsum(row_count, axis=1) - row_count
    first_slot = earlier_rows - before_owner + owner_range[None, :] * capacity
    slot_ids = (
        jnp.sum(matches * first_slot[:, None, :], axis=2)
        + jnp.arange(width_k, dtype=jnp.int32)[None, :]
    )
    flat_slot = slot_ids.reshape(-1)
    requests = jnp.zeros((owners * capacity,), jnp.int32).at[flat_slot].set(local_row.reshape(-1))
    requests = requests.reshape(owners, capacity)
    asked_rows = lax.all_to_all(requests, ("own", "col"), split_axis=0, concat_axis=0, tiled=True)
    fetched = features[asked_rows]
    returned = lax.all_to_all(fetched, ("own", "col"), split_axis=0, concat_axis=0, tiled=True)
    received = returned.reshape(owners * capacity, width_f)
    contract_first = (((0,), (0,)), ((), ()))
    target_ids = jnp.broadcast_to(
        jnp.arange(targets, dtype=jnp.int32)[:, None], (targets, width_k)
    ).reshape(-1)
    spread = (
        jnp.zeros((targets, owners * capacity), jnp.bfloat16)
        .at[target_ids, flat_slot]
        .set(nbr_weight.reshape(-1))
    )
    pre_act = jnp.dot(received, w_one, preferred_element_type=jnp.float32)
    active = jnp.maximum(pre_act, 0.0).astype(jnp.bfloat16)
    hidden = jnp.dot(spread, active, preferred_element_type=jnp.float32).astype(jnp.bfloat16)
    partial_logits = jnp.dot(hidden, w_two, preferred_element_type=jnp.float32)
    logits = lax.psum(partial_logits, "mlp")
    exponent = jnp.exp(logits)
    probability = exponent / jnp.sum(exponent, axis=1, keepdims=True)
    classes = w_two.shape[1]
    onehot_label = (labels[:, None] == jnp.arange(classes, dtype=jnp.int32)[None, :]).astype(
        jnp.float32
    )
    d_logits = (probability - onehot_label).astype(jnp.bfloat16)
    grad_two = lax.dot_general(hidden, d_logits, contract_first, preferred_element_type=jnp.float32)
    d_hidden = lax.dot_general(
        d_logits, w_two, (((1,), (1,)), ((), ())), preferred_element_type=jnp.float32
    ).astype(jnp.bfloat16)
    positive = (pre_act > 0).astype(jnp.float32)
    scattered = lax.dot_general(
        spread, d_hidden, contract_first, preferred_element_type=jnp.float32
    )
    d_pre = (scattered * positive).astype(jnp.bfloat16)
    grad_one = lax.dot_general(received, d_pre, contract_first, preferred_element_type=jnp.float32)
    grad_one, grad_two = lax.psum((grad_one, grad_two), ("own", "col"))
    return (grad_one, grad_two)


def solution(mesh):
    placed = (
        P(("own", "col"), None),
        P(("own", "col"), None),
        P(("own", "col"), None),
        P(("own", "col")),
        P(None, "mlp"),
        P("mlp", None),
    )
    return jax.shard_map(
        body,
        mesh=mesh,
        in_specs=placed,
        out_specs=(P(None, "mlp"), P("mlp", None)),
        check_vma=False,
    )
```

profile of v0, /device:TPU:0, one launch (start us, length us, event | category | flops | bytes accessed | tf_op | source)
XLA Modules:
  0.0 426.2 jit_solution(10001840321477852949)
XLA Ops:
  7.2 0.8 add_select_fusion
  8.1 0.2 reduce_window_sum.23
  8.3 0.2 reduce_window_sum.22
  9.2 15.5 %scatter_custom_fusion = s32[8192]{0:T(1024)S(1)} fusion(s32[4096]{0:T(1024)S(1)} %bitcast.20, s32[4096]{0:T(1024)S(1)} %reshape.163, s32[]{:T(128)} %constant.41.clone.1), kind=kCustom, calls=%fused_computation.33 | custom fusion | bytes 32772 | tf_op jit(solution)/shard_map/scatter | solution.py:28
  24.7 13.7 %all_to_all.17 = s32[8,1,1024]{2,1,0:T(1,128)S(1)} all-to-all(s32[8,1,1024]{2,1,0:T(1,128)S(1)} %bitcast.21), channel_id=1, replica_groups=mesh['own'=4,'col'=2,'mlp'=4] {'own','col'}, dimensions={0} | all-to-all | bytes 65536 | tf_op jit(solution)/shard_map/all_to_all | solution.py:30
  38.5 36.5 %gather_fusion = bf16[8192,512]{1,0:T(8,128)(2,1)} fusion(bf16[4096,512]{1,0:T(8,128)(2,1)} %param.6, s32[8192]{0:T(1024)S(1)} %broadcast_clamp_fusion), kind=kCustom, calls=%fused_computation | custom fusion | bytes 16809984 | tf_op jit(solution)/shard_map/gather | solution.py:31
  75.0 5.1 %all-to-all-start.1 = ((bf16[8,1024,512]{2,1,0:T(8,128)(2,1)}), bf16[8,1024,512]{2,1,0:T(8,128)(2,1)}, u32[]{:S(2)}, u32[]{:S(2)}) async-start(bf16[8,1024,512]{2,1,0:T(8,128)(2,1)} %bitcast.19), calls=%async_computation.1 | async-start | bytes 16777216 | tf_op jit(solution)/shard_map/all_to_all | solution.py:32
  80.6 0.1 and_reduce_fusion
  80.7 30.4 %scatter_custom_fusion.1 = bf16[1048576]{0:T(1024)(128)(2,1)} fusion(s32[4096]{0:T(1024)S(1)} %broadcast_select_fusion, bf16[4096]{0:T(1024)(128)(2,1)S(1)} %reshape.169, bf16[]{:T(256)} %constant.50.clone.1), kind=kCustom, calls=%fused_computation.10 | custom fusion | bytes 2097154
  111.1 2.8 reshape.150
  113.9 148.1 %all-to-all-done.1 = bf16[8,1024,512]{2,1,0:T(8,128)(2,1)} async-done(((bf16[8,1024,512]{2,1,0:T(8,128)(2,1)}), bf16[8,1024,512]{2,1,0:T(8,128)(2,1)}, u32[]{:S(2)}, u32[]{:S(2)}) %all-to-all-start.1) | async-done | bytes 8388640 | tf_op jit(solution)/shard_map/all_to_all | solution.py:32
  262.1 7.1 %fusion.13 = f32[8192,512]{1,0:T(8,128)S(1)} fusion(bf16[8192,512]{1,0:T(8,128)(2,1)} %bitcast.5, bf16[512,512]{1,0:T(8,128)(2,1)S(1)} %copy-done), kind=kOutput, calls=%fused_computation.42 | convolution fusion | flops 4294967296 | bytes 25690112 | tf_op jit(solution)/shard_map/dot_general | solution.py:43
  269.2 1.6 fusion.3
  270.8 4.1 copy-done.1
  274.9 0.8 fusion.14
  275.7 0.2 all-reduce.6.cloned.1.call-start
  276.0 30.4 %all-reduce.4.cloned.1.call-done = f32[128,256]{1,0:T(8,128)} async-done(((f32[128,256]{1,0:T(8,128)}), f32[128,256]{1,0:T(8,128)}) %all-reduce.4.cloned.1.call-update) | async-done | bytes 131088 | tf_op jit(solution)/shard_map/psum | solution.py:47
  306.3 1.0 exponential_reduce_fusion
  307.4 1.1 convolution_convert_fusion
  308.5 16.1 %fusion.2 = f32[512,512]{1,0:T(8,128)} fusion(bf16[8192,512]{1,0:T(8,128)(2,1)} %bitcast.5, f32[8192,512]{1,0:T(8,128)} %copy-done.1, bf16[128,8192]{1,0:T(8,128)(2,1)S(1)} %reshape.150, bf16[128,512]{1,0:T(8,128)(2,1)S(1)} %convolution_convert_fusion), kind=kOutput, calls=%fused_computation.7 | convolution fusion | flops 5381292032 | bytes 28442624 | tf_op jit(solution)/shard_map/dot_general | solution.py:64
  324.6 1.1 fusion.12
  325.7 89.5 %all-reduce.6.cloned.1.call-done = (f32[512,512]{1,0:T(8,128)}, f32[512,256]{1,0:T(8,128)}) async-done(((f32[512,512]{1,0:T(8,128)}, f32[512,256]{1,0:T(8,128)}), (f32[512,512]{1,0:T(8,128)}, f32[512,256]{1,0:T(8,128)})) %all-reduce.6.cloned.1.call-update) | async-done | bytes 1572880 | tf_op jit(solution)/shard_map/psum | solution.py:65
  415.2 2.3 copy.23
  417.5 1.9 copy.24
  (38 shorter events, 1.3 us)
Async XLA Ops:
  7.2 254.9 %copy-start = (bf16[512,512]{1,0:T(8,128)(2,1)S(1)}, bf16[512,512]{1,0:T(8,128)(2,1)}, u32[]{:S(2)}) copy-start(bf16[512,512]{1,0:T(8,128)(2,1)} %param.10) | copy-start | bytes 1572868
  75.0 5.2 %copy-start.4 = (bf16[128,32]{0,1:T(8,128)(2,1)S(1)}, bf16[128,32]{0,1:T(8,128)(2,1)}, u32[]{:S(2)}) copy-start(bf16[128,32]{0,1:T(8,128)(2,1)} %param.8) | copy-start | bytes 24580
  75.0 5.4 %copy-start.7 = (s32[2]{0:T(128)S(1)}, s32[2]{0:T(128)}, u32[]{:S(2)}) copy-start(s32[2]{0:T(128)} %constant.52) | copy-start | bytes 28
  75.0 5.5 %copy-start.6 = (s32[2]{0:T(128)S(1)}, s32[2]{0:T(128)}, u32[]{:S(2)}) copy-start(s32[2]{0:T(128)} %constant.55) | copy-start | bytes 28
  75.0 187.0 %all-to-all-start.1 = ((bf16[8,1024,512]{2,1,0:T(8,128)(2,1)}), bf16[8,1024,512]{2,1,0:T(8,128)(2,1)}, u32[]{:S(2)}, u32[]{:S(2)}) async-start(bf16[8,1024,512]{2,1,0:T(8,128)(2,1)} %bitcast.19), calls=%async_computation.1 | async-start | bytes 16777216 | tf_op jit(solution)/shard_map/all_to_all | solution.py:32
  80.2 226.2 %all-reduce.4.cloned.1.call-start = ((), (), s32[]{:S(2)}) async-start(), calls=%async_computation.2 | async-start | bytes 262144 | tf_op jit(solution)/shard_map/psum | solution.py:47
  269.1 5.7 %copy-start.1 = (f32[8192,512]{1,0:T(8,128)}, f32[8192,512]{1,0:T(8,128)S(1)}, u32[]{:S(2)}) copy-start(f32[8192,512]{1,0:T(8,128)S(1)} %fusion.13) | copy-start | bytes 50331652
  269.2 5.7 %copy-start.3 = (bf16[512,256]{1,0:T(8,128)(2,1)S(1)}, bf16[512,256]{1,0:T(8,128)(2,1)}, u32[]{:S(2)}) copy-start(bf16[512,256]{1,0:T(8,128)(2,1)} %param.11) | copy-start | bytes 786436
  269.2 38.2 %copy-start.5 = (s32[128]{0:T(128)S(1)}, s32[128]{0:T(128)}, u32[]{:S(2)}) copy-start(s32[128]{0:T(128)} %param.9) | copy-start | bytes 1540
  275.7 139.5 %all-reduce.6.cloned.1.call-start = ((), (), s32[]{:S(2)}) async-start(), calls=%async_computation.3 | async-start | bytes 3145728 | tf_op jit(solution)/shard_map/psum | solution.py:65
  308.5 16.1 %copy-start.2 = (f32[128,256]{1,0:T(8,128)S(1)}, f32[128,256]{1,0:T(8,128)}, u32[]{:S(2)}) copy-start(f32[128,256]{1,0:T(8,128)} %all-reduce.4.cloned.1.call-done) | copy-start | bytes 393220
Sparse Core Ops, SparseCore 0:
  275.9 30.4 all-reduce.3
  325.9 89.3 all-reduce.5
where the time goes:
time: 427 us; the launch traced here: 426 us
  waiting for transfers between devices  268 us (63%)
  local copies, waits for them, and re-layouts  94.4 us (22%)
  matrix products  27.8 us (7%)
  between operations  14.3 us (3%)
  blocking collectives  13.7 us (3%)
  starting transfers between devices  5.37 us (1%)
    all_to_all x1, waiting for transfers between devices, body(): lax.all_to_all(fetched, ('own', 'col'), split_axis=0, concat_axis=0, tile...  148 us
    psum x1, waiting for transfers between devices, body(): grad_one, grad_two = lax.psum((grad_one, grad_two), ('own', 'col'))  89.5 us
    unnamed x20, local copies, waits for them, and re-layouts  38.8 us
    gather x1, local copies, waits for them, and re-layouts, body(): fetched = features[asked_rows]  36.5 us
    psum x1, waiting for transfers between devices, body(): logits = lax.psum(partial_logits, 'mlp')  30.4 us
    dot_general x1, matrix products, body(): lax.dot_general(received, d_pre, contract_first, preferred_element_type=j...  16.1 us
    scatter x1, local copies, waits for them, and re-layouts, body(): jnp.zeros((owners * capacity,), jnp.int32).at[flat_slot]  15.5 us
    all_to_all x1, blocking collectives, body(): lax.all_to_all(requests, ('own', 'col'), split_axis=0, concat_axis=0, til...  13.7 us
  transfers between devices with their start and end apart: 3, of which 3 were waited for; matrix products, arithmetic and copies ran while one was open for 8% of the time, Pallas kernels for 0%

commit v1 on v0

v1 whole, which is shorter than its diff:
```python
import functools
import jax
import jax.numpy as jnp
from jax import lax
from jax.experimental import pallas as pl
from jax.experimental.pallas import tpu as pltpu
from jax.sharding import PartitionSpec as P

GROUP = 8
LOW = 256
NT = (((1,), (1,)), ((), ()))
VMEM_LIMIT = 56 * 1024 * 1024


def dot(a, b):
    return jnp.dot(a, b, preferred_element_type=jnp.float32)


def dot_nt(a, b):
    return lax.dot_general(a, b, NT, preferred_element_type=jnp.float32)


def build_spread(page_ref, weight_ref, first_row, rows_dev, spread_ref, chunk):
    span = page_ref.shape[1]
    width_k = span // GROUP
    high = rows_dev // LOW
    local = page_ref[...] - first_row
    here = (local >= 0) & (local < rows_dev)
    lane_target = lax.broadcasted_iota(jnp.int32, local.shape, 1) // width_k
    key = jnp.where(here, (local // LOW) * GROUP + lane_target, -1).astype(jnp.float32)
    low = jnp.where(here, local % LOW, -1).astype(jnp.float32)
    key = key.astype(jnp.bfloat16)
    low = low.astype(jnp.bfloat16)
    weight = weight_ref[...]
    zero = jnp.zeros((), jnp.bfloat16)
    one = jnp.ones((), jnp.bfloat16)
    key_rows = lax.broadcasted_iota(jnp.int32, (high * GROUP, span), 0).astype(jnp.float32).astype(jnp.bfloat16)
    low_rows = lax.broadcasted_iota(jnp.int32, (LOW, span), 0).astype(jnp.float32).astype(jnp.bfloat16)
    for pair in range(chunk // (2 * GROUP)):
        parts = []
        for g in (2 * pair, 2 * pair + 1):
            left = jnp.where(key_rows == key[g : g + 1, :], weight[g : g + 1, :], zero)
            right = jnp.where(low_rows == low[g : g + 1, :], one, zero)
            parts.append(dot_nt(left, right))
        for h in range(high):
            rows = [p[h * GROUP : (h + 1) * GROUP, :] for p in parts]
            spread_ref[2 * GROUP * pair : 2 * GROUP * (pair + 1), h * LOW : (h + 1) * LOW] = (
                jnp.concatenate(rows, axis=0).astype(jnp.bfloat16)
            )


def forward_kernel(own_axes, page_ref, weight_ref, feat_ref, w_one_t_ref, w_two_t_ref,
                   active_ref, spread_ref, hidden_ref, logit_ref):
    rows_dev = feat_ref.shape[0]
    chunk = spread_ref.shape[0]
    first_row = lax.axis_index(own_axes) * rows_dev

    @pl.when(pl.program_id(0) == 0)
    def _():
        def tile(i, _):
            at = pl.ds(pl.multiple_of(i * 512, 512), 512)
            pre = dot_nt(w_one_t_ref[...], feat_ref[at, :])
            active_ref[:, at] = jnp.maximum(pre, 0.0).astype(jnp.bfloat16)
            return 0
        lax.fori_loop(0, rows_dev // 512, tile, 0)

    build_spread(page_ref, weight_ref, first_row, rows_dev, spread_ref, chunk)
    hidden = dot_nt(active_ref[...], spread_ref[...]).astype(jnp.bfloat16)
    hidden_ref[...] = hidden
    logit_ref[...] = dot(w_two_t_ref[...], hidden)


def forward(own_axes, pages, weights, features, w_one_t, w_two_t):
    rows_dev, width_f = features.shape
    units = w_one_t.shape[0]
    classes = w_two_t.shape[0]
    groups, span = pages.shape
    targets = groups * GROUP
    chunk = min(256, targets)
    steps = targets // chunk
    whole = lambda shape: pl.BlockSpec(shape, lambda i: (0, 0))
    return pl.pallas_call(
        functools.partial(forward_kernel, own_axes),
        grid=(steps,),
        in_specs=[
            pl.BlockSpec((chunk // GROUP, span), lambda i: (i, 0)),
            pl.BlockSpec((chunk // GROUP, span), lambda i: (i, 0)),
            whole((rows_dev, width_f)),
            whole((units, width_f)),
            whole((classes, units)),
        ],
        out_specs=[
            whole((units, rows_dev)),
            pl.BlockSpec((chunk, rows_dev), lambda i: (i, 0)),
            pl.BlockSpec((units, chunk), lambda i: (0, i)),
            pl.BlockSpec((classes, chunk), lambda i: (0, i)),
        ],
        out_shape=[
            jax.ShapeDtypeStruct((units, rows_dev), jnp.bfloat16),
            jax.ShapeDtypeStruct((targets, rows_dev), jnp.bfloat16),
            jax.ShapeDtypeStruct((units, targets), jnp.bfloat16),
            jax.ShapeDtypeStruct((classes, targets), jnp.float32),
        ],
        compiler_params=pltpu.CompilerParams(vmem_limit_bytes=VMEM_LIMIT),
    )(pages, weights, features, w_one_t, w_two_t)


def backward_kernel(dlog_ref, hidden_ref, w_two_ref, spread_ref, active_ref, feat_ref,
                    grad_one_ref, grad_two_ref, d_hidden, total):
    step = pl.program_id(0)

    @pl.when(step == 0)
    def _():
        d_hidden[...] = dot(w_two_ref[...], dlog_ref[...]).astype(jnp.bfloat16)
        grad_two_ref[...] = dot_nt(hidden_ref[...], dlog_ref[...])
        total[...] = jnp.zeros_like(total)

    spread_grad = dot(d_hidden[...], spread_ref[...])
    d_pre = jnp.where(active_ref[...] > 0, spread_grad, 0.0).astype(jnp.bfloat16)
    total[...] += dot(d_pre, feat_ref[...])

    @pl.when(step == pl.num_programs(0) - 1)
    def _():
        grad_one_ref[...] = total[...].T


def backward(dlog_t, hidden_t, w_two, spread, active_t, features):
    rows_dev, width_f = features.shape
    units, classes = w_two.shape
    targets = spread.shape[0]
    block = 512
    whole = lambda shape: pl.BlockSpec(shape, lambda i: (0, 0))
    return pl.pallas_call(
        backward_kernel,
        grid=(rows_dev // block,),
        in_specs=[
            whole((classes, targets)),
            whole((units, targets)),
            whole((units, classes)),
            pl.BlockSpec((targets, block), lambda i: (0, i)),
            pl.BlockSpec((units, block), lambda i: (0, i)),
            pl.BlockSpec((block, width_f), lambda i: (i, 0)),
        ],
        out_specs=[whole((width_f, units)), whole((units, classes))],
        out_shape=[
            jax.ShapeDtypeStruct((width_f, units), jnp.float32),
            jax.ShapeDtypeStruct((units, classes), jnp.float32),
        ],
        scratch_shapes=[
            pltpu.VMEM((units, targets), jnp.bfloat16),
            pltpu.VMEM((units, width_f), jnp.float32),
        ],
        compiler_params=pltpu.CompilerParams(vmem_limit_bytes=VMEM_LIMIT),
    )(dlog_t, hidden_t, w_two, spread, active_t, features)


def body(features, nbr_page, nbr_weight, labels, w_one, w_two):
    own_axes = ("own", "col")
    targets_dev, width_k = nbr_page.shape
    span = GROUP * width_k
    pages = lax.all_gather(nbr_page.reshape(-1, span), own_axes, axis=0, tiled=True)
    weights = lax.all_gather(nbr_weight.reshape(-1, span), own_axes, axis=0, tiled=True)
    all_labels = lax.all_gather(labels, own_axes, axis=0, tiled=True)
    active_t, spread, hidden_t, part_t = forward(own_axes, pages, weights, features, w_one.T, w_two.T)
    logits = lax.psum(part_t, ("own", "col", "mlp"))
    exponent = jnp.exp(logits)
    probability = exponent / jnp.sum(exponent, axis=0, keepdims=True)
    classes = w_two.shape[1]
    onehot = (jnp.arange(classes, dtype=jnp.int32)[:, None] == all_labels[None, :]).astype(jnp.float32)
    dlog_t = (probability - onehot).astype(jnp.bfloat16)
    grad_one, grad_two = backward(dlog_t, hidden_t, w_two, spread, active_t, features)
    return lax.psum((grad_one, grad_two), own_axes)


def solution(mesh):
    placed = (
        P(("own", "col"), None),
        P(("own", "col"), None),
        P(("own", "col"), None),
        P(("own", "col")),
        P(None, "mlp"),
        P("mlp", None),
    )
    return jax.shard_map(
        body,
        mesh=mesh,
        in_specs=placed,
        out_specs=(P(None, "mlp"), P("mlp", None)),
        check_vma=False,
    )
```

time: 427 us -> 349 us (0.82)
  local copies, waits for them, and re-layouts: 94.4 us -> 9.78 us
  blocking collectives: 13.7 us -> 87.1 us
  waiting for transfers between devices: 268 us -> 199 us
  Pallas kernels: 0 us -> 35.2 us
  matrix products: 27.8 us -> 0 us
  starting transfers between devices: 5.37 us -> 0.08 us
    all_to_all x1 -> x0, waiting for transfers between devices: 148 us -> none  [body(): lax.all_to_all(fetched, ('own', 'col'), split_axis=0, concat_axis=0, tile...]
    all_gather x0 -> x3, blocking collectives: none -> 87.1 us  [the longest x1 34.3 us: body(): lax.all_gather(nbr_page.reshape(-1, span), own_axes, axis=0, tiled=True)]
    psum x2, waiting for transfers between devices: 120 us -> 199 us  [the longest x1 111 us: body(): logits = lax.psum(part_t, ('own', 'col', 'mlp'))]
    gather x1 -> x0, local copies, waits for them, and re-layouts: 36.5 us -> none  [body(): fetched = features[asked_rows]]
    pallas_call x0 -> x2, Pallas kernels: none -> 35.2 us  [the longest x1 20.7 us: forward(): pl.pallas_call(functools.partial(forward_kernel, own_axes), grid=(steps,)...]
    unnamed x20 -> x8, local copies, waits for them, and re-layouts: 38.8 us -> 9.6 us
    dot_general x6 -> x0, matrix products: 27.8 us -> none  [the longest x1 16.1 us: body(): lax.dot_general(received, d_pre, contract_first, preferred_element_type=j...]
    scatter x2 -> x0, local copies, waits for them, and re-layouts: 18.4 us -> none  [the longest x1 15.5 us: body(): jnp.zeros((owners * capacity,), jnp.int32).at[flat_slot]]
  transfers between devices with their start and end apart: 3 -> 2, of which waited for: 3 -> 2; matrix products, arithmetic and copies ran while one was open for 8% -> 0% of each run, Pallas kernels for 0% -> 0%
where the time goes in v1:
time: 349 us
  waiting for transfers between devices  199 us (57%)
  blocking collectives  87.1 us (25%)
  Pallas kernels  35.2 us (10%)
  between operations  14.1 us (4%)
  local copies, waits for them, and re-layouts  9.78 us (3%)
  other arithmetic  3.66 us (1%)
    psum x1, waiting for transfers between devices, body(): logits = lax.psum(part_t, ('own', 'col', 'mlp'))  111 us
    psum x1, waiting for transfers between devices, body(): return lax.psum((grad_one, grad_two), own_axes)  88.4 us
    all_gather x1, blocking collectives, body(): lax.all_gather(nbr_page.reshape(-1, span), own_axes, axis=0, tiled=True)  34.3 us
    all_gather x1, blocking collectives, body(): lax.all_gather(nbr_weight.reshape(-1, span), own_axes, axis=0, tiled=True)  32.4 us
    pallas_call x1, Pallas kernels, forward(): pl.pallas_call(functools.partial(forward_kernel, own_axes), grid=(steps,)...  20.7 us
    all_gather x1, blocking collectives, body(): all_labels = lax.all_gather(labels, own_axes, axis=0, tiled=True)  20.3 us
    pallas_call x1, Pallas kernels, backward(): pl.pallas_call(backward_kernel, grid=(rows_dev // block,), in_specs=[whol...  14.4 us
    unnamed x8, local copies, waits for them, and re-layouts  9.6 us
  transfers between devices with their start and end apart: 2, of which 2 were waited for; matrix products, arithmetic and copies ran while one was open for 0% of the time, Pallas kernels for 0%

profile of v1, /device:TPU:0, one launch (start us, length us, event | category | flops | bytes accessed | tf_op | source)
XLA Modules:
  0.0 348.8 jit_solution(12187671453767698067)
XLA Ops:
  7.2 0.0 copy-start
  7.2 0.0 all-reduce.4.cloned.1.call-start
  7.2 2.0 copy.18
  9.3 1.8 copy.19
  11.1 0.8 copy.16
  11.9 0.1 reshape.12
  12.0 34.3 %all_gather.9.page_ref = s32[128,256]{1,0:T(8,128)} all-gather(s32[16,256]{1,0:T(8,128)S(1)} %reshape.12), channel_id=1, replica_groups=mesh['own'=4,'col'=2,'mlp'=4] {'own','col'}, dimensions={0}, use_global_device_ids=true | all-gather | bytes 147456 | tf_op jit(solution)/shard_map/all_gather | solution.py:161
  46.3 0.8 copy.17
  47.1 0.1 reshape.13
  47.2 32.4 %all_gather.10.weight_ref = bf16[128,256]{1,0:T(8,128)(2,1)} all-gather(bf16[16,256]{1,0:T(8,128)(2,1)S(1)} %reshape.13), channel_id=1, replica_groups=mesh['own'=4,'col'=2,'mlp'=4] {'own','col'}, dimensions={0}, use_global_device_ids=true | all-gather | bytes 73728 | tf_op jit(solution)/shard_map/all_gather | solution.py:162
  79.6 20.7 %shard_map.77 = (bf16[512,4096]{1,0:T(8,128)(2,1)}, bf16[1024,4096]{1,0:T(8,128)(2,1)}, bf16[512,1024]{1,0:T(8,128)(2,1)}, f32[256,1024]{1,0:T(8,128)}) custom-call(s32[128,256]{1,0:T(8,128)} %all_gather.9.page_ref, bf16[128,256]{1,0:T(8,128)(2,1)} %all_gather.10.weight_ref, bf16[4096,512]{1,0:T(8,128)(2,1)} %feat_ref.3, bf16[512,512]{1,0:T(8,128)(2,1)} %bitcast.4, ...), custom_call_target="tpu_custom_call" | custom-call | tf_op jit(solution)/shard_map/pallas_call | solution.py:82
  100.3 0.0 all-reduce.4.cloned.1.call-update
  100.4 0.0 all-reduce.6.cloned.1.call-start
  100.4 0.0 copy-done
  100.4 20.3 %all-gather = s32[8,1,128]{2,1,0:T(1,128)S(1)} all-gather(s32[1,1,128]{2,1,0:T(1,128)S(1)} %bitcast.7), channel_id=1, replica_groups=mesh['own'=4,'col'=2,'mlp'=4] {'own','col'}, dimensions={0}, use_global_device_ids=true | all-gather | bytes 4608 | tf_op jit(solution)/shard_map/all_gather | solution.py:163
  120.8 110.5 %all-reduce.4.cloned.1.call-done = f32[256,1024]{1,0:T(8,128)} async-done(((f32[256,1024]{1,0:T(8,128)}), f32[256,1024]{1,0:T(8,128)}) %all-reduce.4.cloned.1.call-update) | async-done | bytes 1048592 | tf_op jit(solution)/shard_map/psum | solution.py:165
  231.3 1.4 exponential_reduce_fusion
  232.7 2.3 subtract_convert_fusion.dlog_ref
  234.9 14.4 %shard_map.78 = (f32[512,512]{1,0:T(8,128)}, f32[512,256]{1,0:T(8,128)}) custom-call(bf16[256,1024]{1,0:T(8,128)(2,1)} %subtract_convert_fusion.dlog_ref, bf16[512,1024]{1,0:T(8,128)(2,1)} %get-tuple-element.9.hidden_ref, bf16[512,256]{1,0:T(8,128)(2,1)} %w_two_ref.1, bf16[1024,4096]{1,0:T(8,128)(2,1)} %get-tuple-element.10.spread_ref, ...), custom_call_target="tpu_custom_call" | custom-call | tf_op jit(solution)/shard_map/pallas_call | solution.py:133
  249.4 0.0 all-reduce.6.cloned.1.call-update
  249.4 88.4 %all-reduce.6.cloned.1.call-done = (f32[512,512]{1,0:T(8,128)}, f32[512,256]{1,0:T(8,128)}) async-done(((f32[512,512]{1,0:T(8,128)}, f32[512,256]{1,0:T(8,128)}), (f32[512,512]{1,0:T(8,128)}, f32[512,256]{1,0:T(8,128)})) %all-reduce.6.cloned.1.call-update) | async-done | bytes 1572880 | tf_op jit(solution)/shard_map/psum | solution.py:172
  337.8 2.3 copy.23
  340.1 1.9 copy.24
Async XLA Ops:
  7.2 93.3 %copy-start = (s32[128]{0:T(128)S(1)}, s32[128]{0:T(128)}, u32[]{:S(2)}) copy-start(s32[128]{0:T(128)} %param.9) | copy-start | bytes 1540
  7.2 224.1 %all-reduce.4.cloned.1.call-start = ((), (), s32[]{:S(2)}) async-start(), calls=%async_computation | async-start | bytes 2097152 | tf_op jit(solution)/shard_map/psum | solution.py:165
  100.4 237.4 %all-reduce.6.cloned.1.call-start = ((), (), s32[]{:S(2)}) async-start(), calls=%async_computation.1 | async-start | bytes 3145728 | tf_op jit(solution)/shard_map/psum | solution.py:172
Sparse Core Ops, SparseCore 0:
  100.5 130.7 all-reduce.3
  249.5 88.2 all-reduce.5

commit v2 on v1

--- a/solution.py
+++ b/solution.py
@@ -8,6 +8,7 @@
 
 GROUP = 8
 LOW = 256
+LANES = 128
 NT = (((1,), (1,)), ((), ()))
 VMEM_LIMIT = 56 * 1024 * 1024
 
@@ -18,6 +19,197 @@
 
 def dot_nt(a, b):
     return lax.dot_general(a, b, NT, preferred_element_type=jnp.float32)
+
+
+MESH = pl.DeviceIdType.MESH
+
+
+def split_axis(axis, parts):
+    size = lax.axis_size(axis)
+    steps, stride = [], 1
+    for members in parts:
+        members = size // stride if members is None else min(members, size // stride)
+        if members > 1:
+            steps.append((axis, members, stride))
+        stride *= members
+    return steps
+
+
+def place(step):
+    axis, members, stride = step
+    return lax.rem(lax.div(lax.axis_index(axis), stride), members)
+
+
+def partner(step, shift):
+    axis, members, stride = step
+    mine = place(step)
+    other = lax.rem(mine + shift, members)
+    return other, {axis: lax.axis_index(axis) + (other - mine) * stride}
+
+
+def greet(steps):
+    barrier = pltpu.get_barrier_semaphore()
+    count = 0
+    for step in steps:
+        for shift in range(1, step[1]):
+            pl.semaphore_signal(barrier, inc=1, device_id=partner(step, shift)[1], device_id_type=MESH)
+            count += 1
+    pl.semaphore_wait(barrier, count)
+
+
+def start_scatter(step, piece, held, recv, sems, started):
+    copies = []
+    for shift in range(1, step[1]):
+        other, device = partner(step, shift)
+        copy = pltpu.make_async_remote_copy(
+            src_ref=held.at[piece, :, other], dst_ref=recv.at[piece, shift - 1],
+            send_sem=sems[0].at[piece, shift - 1], recv_sem=sems[1].at[piece, shift - 1],
+            device_id=device, device_id_type=MESH)
+        copy.start()
+        copies.append(copy)
+    started.extend(copies)
+    return copies
+
+
+def start_gather(steps, k, piece, full, sems, started):
+    where = (piece,) + (slice(None),) * (len(steps) - 1 - k) + tuple(place(s) for s in reversed(steps[: k + 1]))
+    copies = []
+    for shift in range(1, steps[k][1]):
+        copy = pltpu.make_async_remote_copy(
+            src_ref=full.at[where], dst_ref=full.at[where],
+            send_sem=sems[0].at[piece, shift - 1], recv_sem=sems[1].at[piece, shift - 1],
+            device_id=partner(steps[k], shift)[1], device_id_type=MESH)
+        copy.start()
+        copies.append(copy)
+    started.extend(copies)
+    return copies
+
+
+def settle(copies):
+    for copy in copies:
+        copy.wait_recv()
+
+
+def sum_kernel(steps, pieces, finish, n_extra, *refs):
+    first = refs[0]
+    extra = refs[1 : 1 + n_extra]
+    full = refs[1 + n_extra]
+    scratch = refs[2 + n_extra :]
+    count = len(steps)
+    recv, held = scratch[:count], (first,) + scratch[count : 2 * count - 1]
+    sems = scratch[2 * count - 1 :]
+    scatter_sems = [(sems[2 * k], sems[2 * k + 1]) for k in range(count)]
+    gather_sems = [(sems[2 * (count + k)], sems[2 * (count + k) + 1]) for k in range(count)]
+    greet(steps)
+    started = []
+    flying = [start_scatter(steps[0], p, held[0], recv[0], scatter_sems[0], started) for p in range(pieces)]
+    last = []
+    for k in range(count):
+        following = []
+        for p in range(pieces):
+            settle(flying[p])
+            total = held[k][p, :, place(steps[k])].astype(jnp.float32)
+            for j in range(steps[k][1] - 1):
+                total = total + recv[k][p, j].astype(jnp.float32)
+            if k + 1 < count:
+                held[k + 1][p] = total.astype(jnp.bfloat16).reshape(held[k + 1].shape[1:])
+                following.append(start_scatter(steps[k + 1], p, held[k + 1], recv[k + 1], scatter_sems[k + 1], started))
+            else:
+                last.append(total.reshape(total.shape[1:]))
+                if finish is None:
+                    full[(p,) + tuple(place(s) for s in reversed(steps))] = last[p].astype(jnp.bfloat16)
+                    following.append(start_gather(steps, k, p, full, gather_sems[k], started))
+        flying = following
+    if finish is not None:
+        results = finish(last, *extra)
+        for p in range(pieces):
+            full[(p,) + tuple(place(s) for s in reversed(steps))] = results[p].astype(jnp.bfloat16)
+            flying.append(start_gather(steps, count - 1, p, full, gather_sems[count - 1], started))
+    for k in range(count - 2, -1, -1):
+        following = []
+        for p in range(pieces):
+            settle(flying[p])
+            following.append(start_gather(steps, k, p, full, gather_sems[k], started))
+        flying = following
+    for p in range(pieces):
+        settle(flying[p])
+    for copy in started:
+        copy.wait_send()
+
+
+def sum_blocks(array, steps, collective_id, finish=None, extra=()):
+    pieces, rows, lanes = array.shape
+    sizes = [s[1] for s in steps]
+    block = rows
+    for size in sizes:
+        block //= size
+    recv, held, outer = [], [], rows // block
+    for k, size in enumerate(sizes):
+        outer //= size
+        if k == 0:
+            first = array.reshape(pieces, outer, size, block, lanes)
+        else:
+            held.append(pltpu.VMEM((pieces, outer, size, block, lanes), jnp.bfloat16))
+        recv.append(pltpu.VMEM((pieces, size - 1, outer, block, lanes), jnp.bfloat16))
+    sems = [pltpu.SemaphoreType.DMA((pieces, size - 1)) for size in sizes for _ in range(2)] * 2
+    vmem = pl.BlockSpec(memory_space=pltpu.VMEM)
+    full = pl.pallas_call(
+        functools.partial(sum_kernel, steps, pieces, finish, len(extra)),
+        in_specs=[vmem] * (1 + len(extra)),
+        out_specs=vmem,
+        out_shape=jax.ShapeDtypeStruct((pieces, *reversed(sizes), block, lanes), jnp.bfloat16),
+        scratch_shapes=recv + held + sems,
+        compiler_params=pltpu.CompilerParams(
+            collective_id=collective_id, has_side_effects=True, vmem_limit_bytes=VMEM_LIMIT),
+    )(first, *extra)
+    return full.reshape(pieces, rows, lanes)
+
+
+def gather_kernel(steps, *refs):
+    count = len(refs) // 3
+    ins, outs, sems = refs[:count], refs[count : 2 * count], refs[2 * count :]
+    where = (0,) + tuple(place(s) for s in reversed(steps))
+    greet(steps)
+    started = []
+    for a in range(count):
+        outs[a][where] = ins[a][...]
+    for k in range(len(steps) - 1, -1, -1):
+        flying = []
+        for a in range(count):
+            pair = (sems[a].at[k, 0], sems[a].at[k, 1])
+            flying.extend(start_gather(steps, k, 0, outs[a], pair, started))
+        settle(flying)
+    for copy in started:
+        copy.wait_send()
+
+
+def gather_blocks(arrays, steps, collective_id):
+    sizes = [s[1] for s in steps]
+    vmem = pl.BlockSpec(memory_space=pltpu.VMEM)
+    outs = pl.pallas_call(
+        functools.partial(gather_kernel, steps),
+        in_specs=[vmem] * len(arrays),
+        out_specs=[vmem] * len(arrays),
+        out_shape=[jax.ShapeDtypeStruct((1, *reversed(sizes), *a.shape), a.dtype) for a in arrays],
+        scratch_shapes=[pltpu.SemaphoreType.DMA((len(steps), 2, 1, max(sizes) - 1))] * len(arrays),
+        compiler_params=pltpu.CompilerParams(
+            collective_id=collective_id, has_side_effects=True, vmem_limit_bytes=VMEM_LIMIT),
+    )(*arrays)
+    return [o.reshape(-1, o.shape[-1]) for o in outs]
+
+
+def softmax_gradient(logits, label_ref):
+    lanes = logits[0].shape[1]
+    rows = logits[0].shape[0]
+    start = pl.multiple_of(lax.axis_index("mlp") * rows, rows)
+    label = label_ref[pl.ds(start, rows), :]
+    exponent = [jnp.exp(x) for x in logits]
+    total = sum(jnp.sum(e, axis=1, keepdims=True) for e in exponent)
+    results = []
+    for p, e in enumerate(exponent):
+        category = lax.broadcasted_iota(jnp.int32, e.shape, 1) + p * lanes
+        results.append(e / total - jnp.where(category == label, 1.0, 0.0))
+    return results
 
 
 def build_spread(page_ref, weight_ref, first_row, rows_dev, spread_ref, chunk):
@@ -67,7 +259,10 @@
     build_spread(page_ref, weight_ref, first_row, rows_dev, spread_ref, chunk)
     hidden = dot_nt(active_ref[...], spread_ref[...]).astype(jnp.bfloat16)
     hidden_ref[...] = hidden
-    logit_ref[...] = dot(w_two_t_ref[...], hidden)
+    logits = dot(w_two_t_ref[...], hidden).T.astype(jnp.bfloat16)
+    lanes = logit_ref.shape[2]
+    for p in range(logit_ref.shape[0]):
+        logit_ref[p] = logits[:, p * lanes : (p + 1) * lanes]
 
 
 def forward(own_axes, pages, weights, features, w_one_t, w_two_t):
@@ -93,26 +288,32 @@
             whole((units, rows_dev)),
             pl.BlockSpec((chunk, rows_dev), lambda i: (i, 0)),
             pl.BlockSpec((units, chunk), lambda i: (0, i)),
-            pl.BlockSpec((classes, chunk), lambda i: (0, i)),
+            pl.BlockSpec((classes // LANES, chunk, LANES), lambda i: (0, i, 0)),
         ],
         out_shape=[
             jax.ShapeDtypeStruct((units, rows_dev), jnp.bfloat16),
             jax.ShapeDtypeStruct((targets, rows_dev), jnp.bfloat16),
             jax.ShapeDtypeStruct((units, targets), jnp.bfloat16),
-            jax.ShapeDtypeStruct((classes, targets), jnp.float32),
+            jax.ShapeDtypeStruct((classes // LANES, targets, LANES), jnp.bfloat16),
         ],
         compiler_params=pltpu.CompilerParams(vmem_limit_bytes=VMEM_LIMIT),
     )(pages, weights, features, w_one_t, w_two_t)
 
 
 def backward_kernel(dlog_ref, hidden_ref, w_two_ref, spread_ref, active_ref, feat_ref,
-                    grad_one_ref, grad_two_ref, d_hidden, total):
+                    grad_ref, d_hidden, total):
     step = pl.program_id(0)
+    units = total.shape[0]
+    width_f = total.shape[1]
+    ones = units // LANES
 
     @pl.when(step == 0)
     def _():
-        d_hidden[...] = dot(w_two_ref[...], dlog_ref[...]).astype(jnp.bfloat16)
-        grad_two_ref[...] = dot_nt(hidden_ref[...], dlog_ref[...])
+        d_logits = jnp.concatenate([dlog_ref[p] for p in range(dlog_ref.shape[0])], axis=1)
+        d_hidden[...] = dot_nt(w_two_ref[...], d_logits).astype(jnp.bfloat16)
+        grad_two = dot(hidden_ref[...], d_logits).astype(jnp.bfloat16)
+        for p in range(grad_two.shape[1] // LANES):
+            grad_ref[ones + p] = grad_two[:, p * LANES : (p + 1) * LANES]
         total[...] = jnp.zeros_like(total)
 
     spread_grad = dot(d_hidden[...], spread_ref[...])
@@ -121,55 +322,56 @@
 
     @pl.when(step == pl.num_programs(0) - 1)
     def _():
-        grad_one_ref[...] = total[...].T
-
-
-def backward(dlog_t, hidden_t, w_two, spread, active_t, features):
+        for p in range(ones):
+            grad_ref[p] = total[p * LANES : (p + 1) * LANES, :].T.astype(jnp.bfloat16)
+
+
+def backward(dlog, hidden_t, w_two, spread, active_t, features):
     rows_dev, width_f = features.shape
     units, classes = w_two.shape
+    assert units == width_f
     targets = spread.shape[0]
     block = 512
-    whole = lambda shape: pl.BlockSpec(shape, lambda i: (0, 0))
+    whole = lambda shape: pl.BlockSpec(shape, lambda i: (0,) * len(shape))
+    out = ((units + classes) // LANES, width_f, LANES)
     return pl.pallas_call(
         backward_kernel,
         grid=(rows_dev // block,),
         in_specs=[
-            whole((classes, targets)),
+            whole(dlog.shape),
             whole((units, targets)),
             whole((units, classes)),
             pl.BlockSpec((targets, block), lambda i: (0, i)),
             pl.BlockSpec((units, block), lambda i: (0, i)),
             pl.BlockSpec((block, width_f), lambda i: (i, 0)),
         ],
-        out_specs=[whole((width_f, units)), whole((units, classes))],
-        out_shape=[
-            jax.ShapeDtypeStruct((width_f, units), jnp.float32),
-            jax.ShapeDtypeStruct((units, classes), jnp.float32),
-        ],
+        out_specs=whole(out),
+        out_shape=jax.ShapeDtypeStruct(out, jnp.bfloat16),
         scratch_shapes=[
             pltpu.VMEM((units, targets), jnp.bfloat16),
             pltpu.VMEM((units, width_f), jnp.float32),
         ],
         compiler_params=pltpu.CompilerParams(vmem_limit_bytes=VMEM_LIMIT),
-    )(dlog_t, hidden_t, w_two, spread, active_t, features)
+    )(dlog, hidden_t, w_two, spread, active_t, features)
 
 
 def body(features, nbr_page, nbr_weight, labels, w_one, w_two):
     own_axes = ("own", "col")
+    units, classes = w_two.shape
     targets_dev, width_k = nbr_page.shape
     span = GROUP * width_k
-    pages = lax.all_gather(nbr_page.reshape(-1, span), own_axes, axis=0, tiled=True)
-    weights = lax.all_gather(nbr_weight.reshape(-1, span), own_axes, axis=0, tiled=True)
-    all_labels = lax.all_gather(labels, own_axes, axis=0, tiled=True)
-    active_t, spread, hidden_t, part_t = forward(own_axes, pages, weights, features, w_one.T, w_two.T)
-    logits = lax.psum(part_t, ("own", "col", "mlp"))
-    exponent = jnp.exp(logits)
-    probability = exponent / jnp.sum(exponent, axis=0, keepdims=True)
-    classes = w_two.shape[1]
-    onehot = (jnp.arange(classes, dtype=jnp.int32)[:, None] == all_labels[None, :]).astype(jnp.float32)
-    dlog_t = (probability - onehot).astype(jnp.bfloat16)
-    grad_one, grad_two = backward(dlog_t, hidden_t, w_two, spread, active_t, features)
-    return lax.psum((grad_one, grad_two), own_axes)
+    owner_steps = split_axis("col", (2, None)) + split_axis("own", (None,))
+    all_steps = split_axis("mlp", (2, None)) + owner_steps
+    pages, weights = gather_blocks(
+        (nbr_page.reshape(-1, span), nbr_weight.reshape(-1, span)), owner_steps, 0)
+    active_t, spread, hidden_t, part = forward(own_axes, pages, weights, features, w_one.T, w_two.T)
+    dlog = sum_blocks(part, all_steps, 1, softmax_gradient, (labels[:, None],))
+    grads = backward(dlog, hidden_t, w_two, spread, active_t, features)
+    grads = sum_blocks(grads, owner_steps, 2).astype(jnp.float32)
+    ones = units // LANES
+    grad_one = jnp.concatenate([grads[p] for p in range(ones)], axis=1)
+    grad_two = jnp.concatenate([grads[p] for p in range(ones, grads.shape[0])], axis=1)
+    return grad_one, grad_two
 
 
 def solution(mesh):

time: 349 us -> 120 us (0.34)
  waiting for transfers between devices: 199 us -> 0 us
  blocking collectives: 87.1 us -> 0 us
  Pallas kernels: 35.2 us -> 108 us
  between operations: 14.1 us -> 0.68 us
    psum x2 -> x0, waiting for transfers between devices: 199 us -> none  [the longest x1 111 us: body(): logits = lax.psum(part_t, ('own', 'col', 'mlp'))]
    all_gather x3 -> x0, blocking collectives: 87.1 us -> none  [the longest x1 34.3 us: body(): lax.all_gather(nbr_page.reshape(-1, span), own_axes, axis=0, tiled=True)]
    pallas_call x0 -> x3, Pallas kernels: none -> 74.3 us  [the longest x2 60.6 us: sum_blocks(): pl.pallas_call(functools.partial(sum_kernel, steps, pieces, finish, len(e...]
    unnamed x8 -> x6, local copies, waits for them, and re-layouts: 9.6 us -> 5.5 us
  transfers between devices with their start and end apart: 2 -> 0, of which waited for: 2 -> 0; matrix products, arithmetic and copies ran while one was open for 0% -> 0% of each run, Pallas kernels for 0% -> 0%
where the time goes in v2:
time: 120 us
  Pallas kernels  108 us (90%)
  local copies, waits for them, and re-layouts  9.01 us (8%)
  other arithmetic  1.87 us (2%)
    pallas_call x2, Pallas kernels, sum_blocks(): pl.pallas_call(functools.partial(sum_kernel, steps, pieces, finish, len(e...  60.6 us
    pallas_call x1, Pallas kernels, forward(): pl.pallas_call(functools.partial(forward_kernel, own_axes), grid=(steps,)...  19.7 us
    pallas_call x1, Pallas kernels, backward(): pl.pallas_call(backward_kernel, grid=(rows_dev // block,), in_specs=[whol...  14 us
    pallas_call x1, Pallas kernels, gather_blocks(): pl.pallas_call(functools.partial(gather_kernel, steps), in_specs=[vmem] *...  13.8 us
    unnamed x6, local copies, waits for them, and re-layouts  5.5 us

profile of v2, /device:TPU:0, one launch (start us, length us, event | category | flops | bytes accessed | tf_op | source)
XLA Modules:
  0.0 119.6 jit_solution(16016129048715365179)
XLA Ops:
  0.6 0.0 copy-start
  0.6 0.8 copy.13
  1.5 0.7 reshape.39.refs_0_
  2.2 0.8 copy.14
  3.0 0.7 reshape.40.refs_1_
  3.7 13.8 %shard_map.77 = (s32[1,4,2,16,256]{4,3,2,1,0:T(8,128)}, bf16[1,4,2,16,256]{4,3,2,1,0:T(8,128)(2,1)}) custom-call(s32[16,256]{1,0:T(8,128)} %reshape.39.refs_0_, bf16[16,256]{1,0:T(8,128)(2,1)} %reshape.40.refs_1_), custom_call_target="tpu_custom_call" | custom-call | tf_op jit(solution)/shard_map/pallas_call | solution.py:189
  17.5 2.0 %copy.15 = bf16[512,512]{0,1:T(8,128)(2,1)} copy(bf16[512,512]{1,0:T(8,128)(2,1)} %param.10) | data formatting | bytes 1048576 | tf_op args[4]
  19.5 1.8 %copy.16 = bf16[512,256]{0,1:T(8,128)(2,1)} copy(bf16[512,256]{1,0:T(8,128)(2,1)} %w_two_ref.1) | data formatting | bytes 524288 | tf_op args[5]
  21.3 19.7 %shard_map.78 = (bf16[512,4096]{1,0:T(8,128)(2,1)}, bf16[1024,4096]{1,0:T(8,128)(2,1)}, bf16[512,1024]{1,0:T(8,128)(2,1)}, bf16[2,1024,128]{2,1,0:T(8,128)(2,1)}) custom-call(s32[128,256]{1,0:T(8,128)} %bitcast.25, bf16[128,256]{1,0:T(8,128)(2,1)} %bitcast.26, bf16[4096,512]{1,0:T(8,128)(2,1)} %feat_ref.3, bf16[512,512]{1,0:T(8,128)(2,1)} %bitcast.15, ...), custom_call_target="tpu_custom_call" | custom-call | tf_op jit(solution)/shard_map/pallas_call | solution.py:277
  41.0 0.0 copy-done
  41.0 0.7 copy.17.refs_1_
  41.7 28.4 %shard_map.79 = bf16[2,4,2,2,2,32,128]{6,5,4,3,2,1,0:T(8,128)(2,1)} custom-call(bf16[2,16,2,32,128]{4,3,2,1,0:T(8,128)(2,1)} %bitcast.24, s32[128,1]{1,0:T(8,128)} %copy.17.refs_1_), custom_call_target="tpu_custom_call" | custom-call | tf_op jit(solution)/shard_map/pallas_call | solution.py:156
  70.2 14.0 %shard_map.80 = bf16[6,512,128]{2,1,0:T(8,128)(2,1)} custom-call(bf16[2,1024,128]{2,1,0:T(8,128)(2,1)} %bitcast.16, bf16[512,1024]{1,0:T(8,128)(2,1)} %get-tuple-element.11.hidden_ref, bf16[512,256]{1,0:T(8,128)(2,1)} %w_two_ref.1, bf16[1024,4096]{1,0:T(8,128)(2,1)} %get-tuple-element.12.spread_ref, bf16[512,4096]{1,0:T(8,128)(2,1)} %get-tuple-element.13.active_ref, ...), custom_call_target="tpu_custom_call" | custom-call | tf_op jit(solution)/shard_map/pallas_call | solution.py:337
  84.2 32.1 %shard_map.81 = bf16[6,4,2,64,128]{4,3,2,1,0:T(8,128)(2,1)} custom-call(bf16[6,4,2,64,128]{4,3,2,1,0:T(8,128)(2,1)} %bitcast.14), custom_call_target="tpu_custom_call" | custom-call | tf_op jit(solution)/shard_map/pallas_call | solution.py:156
  116.3 1.4 %fusion = (f32[1,4,2,64,128]{4,3,2,1,0:T(8,128)S(1)}, f32[1,4,2,64,128]{4,3,2,1,0:T(8,128)S(1)}, f32[1,4,2,64,128]{4,3,2,1,0:T(8,128)S(1)}, f32[1,4,2,64,128]{4,...) fusion(bf16[6,4,2,64,128]{4,3,2,1,0:T(8,128)(2,1)} %shard_map.81), kind=kLoop, calls=%fused_computation.2 | loop fusion | bytes 3145728 | tf_op jit(solution)/shard_map/slice | solution.py:373
  117.7 0.8 pad_maximum_fusion.1
  118.6 1.0 pad_maximum_fusion
Async XLA Ops:
  0.6 40.4 %copy-start = (s32[128]{0:T(128)S(1)}, s32[128]{0:T(128)}, u32[]{:S(2)}) copy-start(s32[128]{0:T(128)} %param.9) | copy-start | bytes 1540

commit v3 on v2

--- a/solution.py
+++ b/solution.py
@@ -9,6 +9,7 @@
 GROUP = 8
 LOW = 256
 LANES = 128
+SPREAD_LIMIT = 8 * 1024 * 1024
 NT = (((1,), (1,)), ((), ()))
 VMEM_LIMIT = 56 * 1024 * 1024
 
@@ -355,6 +356,248 @@
     )(dlog, hidden_t, w_two, spread, active_t, features)
 
 
+def scatter_total(step, piece, held, recv):
+    total = held[piece, :, place(step)].astype(jnp.float32)
+    for j in range(step[1] - 1):
+        total = total + recv[piece, j].astype(jnp.float32)
+    return total
+
+
+def advance(running):
+    for task in list(running):
+        if next(task, "done") == "done":
+            running.remove(task)
+
+
+def fused_kernel(plan, *refs):
+    it = iter(refs)
+    packed_ref, label_ref, feat_ref, w_one_ref, w_two_ref, one_ref, two_ref = (next(it) for _ in range(7))
+    pages_all, key_s, low_s, weight_s, active, spread, hidden, d_hidden, total = (next(it) for _ in range(9))
+    inner, own, owner_steps, grad_steps = plan
+    all_steps = inner + own
+    chunks = own[0][1]
+    held = [next(it) for _ in inner]
+    recv = [next(it) for _ in inner]
+    own_held, own_recv, full = (next(it) for _ in range(3))
+    grad_held = [next(it) for _ in grad_steps]
+    grad_recv = [next(it) for _ in grad_steps]
+    grad_full = next(it)
+    pairs = lambda n: [(next(it), next(it)) for _ in range(n)]
+    page_sems = pairs(len(owner_steps))
+    inner_sems = pairs(len(inner))
+    own_sems = pairs(1)[0]
+    full_sems = pairs(len(all_steps))
+    scatter_sems = pairs(len(grad_steps))
+    gather_sems = pairs(len(grad_steps))
+
+    rows_dev, width_f = feat_ref.shape
+    units, classes = w_two_ref.shape
+    targets = spread.shape[0]
+    chunk = targets // chunks
+    span = key_s.shape[1]
+    width_k = span // GROUP
+    high = rows_dev // LOW
+    started = []
+
+    greet(all_steps)
+    pages_all[(0,) + tuple(place(s) for s in reversed(owner_steps))] = packed_ref[...]
+    w_one_t = w_one_ref[...].T
+    stages = len(owner_steps)
+    tiles = rows_dev // 512
+    for k in range(stages - 1, -1, -1):
+        flying = start_gather(owner_steps, k, 0, pages_all, page_sems[k], started)
+        done = stages - 1 - k
+        for i in range(done * tiles // stages, (done + 1) * tiles // stages):
+            pre = dot_nt(w_one_t, feat_ref[i * 512 : (i + 1) * 512, :])
+            active[:, i * 512 : (i + 1) * 512] = jnp.maximum(pre, 0.0).astype(jnp.bfloat16)
+        settle(flying)
+
+    lists = pages_all[0]
+    lead = (slice(None),) * stages
+    page = lists[lead + (0,)].reshape(-1, span)
+    weight_s[...] = lists[lead + (1,)].reshape(-1, span)
+    local = page.astype(jnp.int32) - lax.axis_index(("own", "col")) * rows_dev
+    here = (local >= 0) & (local < rows_dev)
+    lane_target = lax.broadcasted_iota(jnp.int32, local.shape, 1) // width_k
+    key_s[...] = jnp.where(here, (local // LOW) * GROUP + lane_target, -1).astype(jnp.float32)
+    low_s[...] = jnp.where(here, local % LOW, -1).astype(jnp.float32)
+
+    zero = jnp.zeros((), jnp.bfloat16)
+    one = jnp.ones((), jnp.bfloat16)
+    key_rows = lax.broadcasted_iota(jnp.int32, (high * GROUP, span), 0).astype(jnp.float32).astype(jnp.bfloat16)
+    low_rows = lax.broadcasted_iota(jnp.int32, (LOW, span), 0).astype(jnp.float32).astype(jnp.bfloat16)
+
+    def build(i, carry):
+        at = pl.ds(pl.multiple_of(i * 8, 8), 8)
+        key = key_s[at, :].astype(jnp.bfloat16)
+        low = low_s[at, :].astype(jnp.bfloat16)
+        weight = weight_s[at, :].astype(jnp.bfloat16)
+        for pair in range(4):
+            parts = []
+            for g in (2 * pair, 2 * pair + 1):
+                left = jnp.where(key_rows == key[g : g + 1, :], weight[g : g + 1, :], zero)
+                right = jnp.where(low_rows == low[g : g + 1, :], one, zero)
+                parts.append(dot_nt(left, right))
+            rows = pl.ds(pl.multiple_of(i * 64 + pair * 16, 16), 16)
+            for h in range(high):
+                both = [p[h * GROUP : (h + 1) * GROUP, :] for p in parts]
+                spread[rows, h * LOW : (h + 1) * LOW] = jnp.concatenate(both, axis=0).astype(jnp.bfloat16)
+        return carry
+
+    def sum_logits(c):
+        for k, step in enumerate(inner):
+            copies = start_scatter(step, c, held[k], recv[k], inner_sems[k], started)
+            yield
+            settle(copies)
+            part = scatter_total(step, c, held[k], recv[k]).astype(jnp.bfloat16)
+            if k + 1 < len(inner):
+                held[k + 1][c] = part.reshape(held[k + 1].shape[1:])
+            else:
+                own_held[0, 0, c] = part[0]
+
+    running = []
+    w_two_t = w_two_ref[...].T
+    blocks = chunk // 64
+    for c in range(chunks):
+        half = blocks // 2
+        lax.fori_loop(c * blocks, c * blocks + half, build, 0)
+        advance(running)
+        lax.fori_loop(c * blocks + half, (c + 1) * blocks, build, 0)
+        advance(running)
+        block = dot_nt(active[...], spread[c * chunk : (c + 1) * chunk, :]).astype(jnp.bfloat16)
+        hidden[:, c * chunk : (c + 1) * chunk] = block
+        held[0][c] = dot(w_two_t, block).T.astype(jnp.bfloat16).reshape(held[0].shape[1:])
+        advance(running)
+        running.append(sum_logits(c))
+        next(running[-1])
+    while running:
+        advance(running)
+    settle(start_scatter(own[0], 0, own_held, own_recv, own_sems, started))
+    logits = scatter_total(own[0], 0, own_held, own_recv)[0]
+    d_logits = softmax_gradient([logits], label_ref)[0].astype(jnp.bfloat16)
+    full[(0,) + tuple(place(s) for s in reversed(all_steps))] = d_logits
+    for k in range(len(all_steps) - 1, -1, -1):
+        settle(start_gather(all_steps, k, 0, full, full_sems[k], started))
+    d_logits = full[0].reshape(targets, classes)
+
+    def sum_grads(p, values):
+        grad_held[0][p] = values.astype(jnp.bfloat16).reshape(grad_held[0].shape[1:])
+        count = len(grad_steps)
+        for k, step in enumerate(grad_steps):
+            copies = start_scatter(step, p, grad_held[k], grad_recv[k], scatter_sems[k], started)
+            yield
+            settle(copies)
+            part = scatter_total(step, p, grad_held[k], grad_recv[k]).astype(jnp.bfloat16)
+            if k + 1 < count:
+                grad_held[k + 1][p] = part.reshape(grad_held[k + 1].shape[1:])
+        grad_full[(p,) + tuple(place(s) for s in reversed(grad_steps))] = part[0]
+        for k in range(count - 1, -1, -1):
+            copies = start_gather(grad_steps, k, p, grad_full, gather_sems[k], started)
+            yield
+            settle(copies)
+        block = grad_full[p].reshape(width_f, LANES)
+        if p < units // LANES:
+            one_ref[:, p * LANES : (p + 1) * LANES] = block
+        else:
+            q = p - units // LANES
+            two_ref[:, q * LANES : (q + 1) * LANES] = block
+
+    def launch(p, values):
+        running.append(sum_grads(p, values))
+        next(running[-1])
+
+    grad_two = dot(hidden[...], d_logits)
+    for q in range(classes // LANES):
+        launch(units // LANES + q, grad_two[:, q * LANES : (q + 1) * LANES])
+    d_hidden[...] = dot_nt(w_two_ref[...], d_logits).astype(jnp.bfloat16)
+    part_units = 256
+    width_r = 1024
+    for u in range(units // part_units):
+        rows = slice(u * part_units, (u + 1) * part_units)
+        for r in range(rows_dev // width_r):
+            at = slice(r * width_r, (r + 1) * width_r)
+            spread_grad = dot(d_hidden[rows, :], spread[:, at])
+            d_pre = jnp.where(active[rows, at] > 0, spread_grad, 0.0).astype(jnp.bfloat16)
+            product = dot(d_pre, feat_ref[at, :])
+            if r == 0:
+                total[...] = product
+            else:
+                total[...] += product
+            if r % 2 == 1:
+                advance(running)
+        for q in range(part_units // LANES):
+            launch(u * (part_units // LANES) + q, total[q * LANES : (q + 1) * LANES, :].T)
+    while running:
+        advance(running)
+    for copy in started:
+        copy.wait_send()
+
+
+def fused(packed, labels, features, w_one, w_two, owner_steps):
+    inner = split_axis("mlp", (2, None)) + split_axis("col", (2, None))
+    own = split_axis("own", (None,))
+    grad_steps = split_axis("col", (2, None)) + split_axis("own", (2, None))
+    all_steps = inner + own
+    rows_dev, width_f = features.shape
+    units, classes = w_two.shape
+    lists, list_rows, span = packed.shape
+    sizes = lambda steps: [s[1] for s in steps]
+    owners = 1
+    for size in sizes(owner_steps):
+        owners *= size
+    groups = owners * list_rows
+    targets = groups * GROUP
+    chunks = own[0][1]
+    bf16 = lambda *shape: pltpu.VMEM(shape, jnp.bfloat16)
+    f32 = lambda *shape: pltpu.VMEM(shape, jnp.float32)
+
+    def buffers(steps, pieces, outer, *block):
+        held, recv = [], []
+        for size in sizes(steps):
+            outer //= size
+            held.append(bf16(pieces, outer, size, *block))
+            recv.append(bf16(pieces, size - 1, outer, *block))
+        return held, recv
+
+    own_rows = targets // chunks
+    for size in sizes(inner):
+        own_rows //= size
+    pieces = (units + classes) // LANES
+    grad_rows = width_f // owners
+    held, recv = buffers(inner, chunks, targets // chunks // own_rows, own_rows, classes)
+    own_held, own_recv = buffers(own, 1, chunks, own_rows, classes)
+    grad_held, grad_recv = buffers(grad_steps, pieces, owners, grad_rows, LANES)
+
+    def sems(steps, count):
+        return [pltpu.SemaphoreType.DMA((count, s - 1)) for s in sizes(steps) for _ in range(2)]
+
+    scratch = [
+        f32(1, *reversed(sizes(owner_steps)), lists, list_rows, span),
+        f32(groups, span), f32(groups, span), f32(groups, span),
+        bf16(units, rows_dev), bf16(targets, rows_dev), bf16(units, targets), bf16(units, targets),
+        f32(256, width_f),
+        *held, *recv, *own_held, *own_recv,
+        bf16(1, *reversed(sizes(all_steps)), own_rows, classes),
+        *grad_held, *grad_recv,
+        bf16(pieces, *reversed(sizes(grad_steps)), grad_rows, LANES),
+        *sems(owner_steps, 1), *sems(inner, chunks), *sems(own, 1), *sems(all_steps, 1),
+        *sems(grad_steps, pieces), *sems(grad_steps, pieces),
+    ]
+    vmem = pl.BlockSpec(memory_space=pltpu.VMEM)
+    return pl.pallas_call(
+        functools.partial(fused_kernel, (inner, own, owner_steps, grad_steps)),
+        in_specs=[vmem] * 5,
+        out_specs=[vmem] * 2,
+        out_shape=[
+            jax.ShapeDtypeStruct((width_f, units), jnp.bfloat16),
+            jax.ShapeDtypeStruct((units, classes), jnp.bfloat16),
+        ],
+        scratch_shapes=scratch,
+        compiler_params=pltpu.CompilerParams(
+            collective_id=3, has_side_effects=True, vmem_limit_bytes=VMEM_LIMIT),
+    )(packed, labels, features, w_one, w_two)
+
+
 def body(features, nbr_page, nbr_weight, labels, w_one, w_two):
     own_axes = ("own", "col")
     units, classes = w_two.shape
@@ -362,6 +605,11 @@
     span = GROUP * width_k
     owner_steps = split_axis("col", (2, None)) + split_axis("own", (None,))
     all_steps = split_axis("mlp", (2, None)) + owner_steps
+    owners = lax.axis_size(own_axes)
+    if targets_dev * owners * features.shape[0] <= SPREAD_LIMIT:
+        packed = jnp.stack([nbr_page.astype(jnp.float32), nbr_weight.astype(jnp.float32)])
+        one, two = fused(packed.reshape(2, -1, span), labels[:, None], features, w_one, w_two, owner_steps)
+        return one.astype(jnp.float32), two.astype(jnp.float32)
     pages, weights = gather_blocks(
         (nbr_page.reshape(-1, span), nbr_weight.reshape(-1, span)), owner_steps, 0)
     active_t, spread, hidden_t, part = forward(own_axes, pages, weights, features, w_one.T, w_two.T)

time: 120 us -> 109 us (0.908)
  Pallas kernels: 108 us -> 100 us
  local copies, waits for them, and re-layouts: 9.01 us -> 2.45 us
  other arithmetic: 1.87 us -> 5.26 us
    pallas_call x5 -> x1, Pallas kernels: 108 us -> 100 us  [fused(): pl.pallas_call(functools.partial(fused_kernel, (inner, own, owner_steps,...]
    unnamed x6 -> x0, local copies, waits for them, and re-layouts: 5.5 us -> none
    convert_element_type x0 -> x3, other arithmetic: none -> 4.64 us  [the longest x2 3.92 us: body(): return (one.astype(jnp.float32), two.astype(jnp.float32))]
    concatenate x2 -> x0, other arithmetic: 1.87 us -> none  [the longest x1 1.04 us: body(): grad_one = jnp.concatenate([grads[p] for p in range(ones)], axis=1)]
    reshape x2 -> x0, local copies, waits for them, and re-layouts: 1.39 us -> none  [the longest x1 0.7 us: body(): nbr_weight.reshape(-1, span)]
    slice x1 -> x0, local copies, waits for them, and re-layouts: 1.38 us -> none  [body(): grads[p]]
where the time goes in v3:
time: 109 us
  Pallas kernels  100 us (92%)
  other arithmetic  5.26 us (5%)
  local copies, waits for them, and re-layouts  2.45 us (2%)
    pallas_call x1, Pallas kernels, fused(): pl.pallas_call(functools.partial(fused_kernel, (inner, own, owner_steps,...  100 us
    convert_element_type x2, other arithmetic, body(): return (one.astype(jnp.float32), two.astype(jnp.float32))  3.92 us

profile of v3, /device:TPU:0, one launch (start us, length us, event | category | flops | bytes accessed | tf_op | source)
XLA Modules:
  0.0 108.5 jit_solution(12500520145761433503)
XLA Ops:
  0.6 0.7 convert_element_type.10
  1.4 0.1 copy.11
  1.4 0.1 stack.11
  1.5 0.8 copy.12
  2.3 0.1 reshape.10
  2.4 0.6 pad_maximum_fusion.refs_0_
  3.0 1.4 %copy.13.refs_1_ = s32[128,1]{1,0:T(8,128)} copy(s32[128,1]{0,1:T(1,128)} %bitcast.1) | data formatting | bytes 1024 | tf_op jit(solution)/shard_map/broadcast_in_dim | solution.py:611
  4.4 100.1 %shard_map.77 = (bf16[512,512]{1,0:T(8,128)(2,1)}, bf16[512,256]{1,0:T(8,128)(2,1)}) custom-call(f32[2,16,256]{2,1,0:T(8,128)} %pad_maximum_fusion.refs_0_, s32[128,1]{1,0:T(8,128)} %copy.13.refs_1_, bf16[4096,512]{1,0:T(8,128)(2,1)} %refs_2_.1, bf16[512,512]{1,0:T(8,128)(2,1)} %refs_3_.1, bf16[512,256]{1,0:T(8,128)(2,1)} %refs_4_.1), custom_call_target="tpu_custom_call" | custom-call | tf_op jit(solution)/shard_map/pallas_call | solution.py:587
  104.6 2.1 %convert_element_type.11 = f32[512,512]{1,0:T(8,128)} convert(bf16[512,512]{1,0:T(8,128)(2,1)} %get-tuple-element.4) | non-fusion elementwise | flops 262144 | bytes 1572864 | tf_op jit(solution)/shard_map/convert_element_type | solution.py:612
  106.7 1.8 %convert_element_type.12 = f32[512,256]{1,0:T(8,128)} convert(bf16[512,256]{1,0:T(8,128)(2,1)} %get-tuple-element.5) | non-fusion elementwise | flops 131072 | bytes 786432 | tf_op jit(solution)/shard_map/convert_element_type | solution.py:612

commit v4 on v3

--- a/solution.py
+++ b/solution.py
@@ -36,16 +36,35 @@
     return steps
 
 
+def joined(steps):
+    members = 1
+    for step in steps:
+        members *= step[1]
+    return (tuple(steps), members, 0)
+
+
 def place(step):
     axis, members, stride = step
-    return lax.rem(lax.div(lax.axis_index(axis), stride), members)
+    if stride:
+        return lax.rem(lax.div(lax.axis_index(axis), stride), members)
+    mine, weight = 0, 1
+    for part in axis:
+        mine = mine + place(part) * weight
+        weight *= part[1]
+    return mine
 
 
 def partner(step, shift):
     axis, members, stride = step
     mine = place(step)
     other = lax.rem(mine + shift, members)
-    return other, {axis: lax.axis_index(axis) + (other - mine) * stride}
+    if stride:
+        return other, {axis: lax.axis_index(axis) + (other - mine) * stride}
+    device, rest = {}, other
+    for part in axis:
+        device[part[0]] = lax.axis_index(part[0]) + (lax.rem(rest, part[1]) - place(part)) * part[2]
+        rest = lax.div(rest, part[1])
+    return other, device
 
 
 def greet(steps):
@@ -371,11 +390,12 @@
 
 def fused_kernel(plan, *refs):
     it = iter(refs)
-    packed_ref, label_ref, feat_ref, w_one_ref, w_two_ref, one_ref, two_ref = (next(it) for _ in range(7))
-    pages_all, key_s, low_s, weight_s, active, spread, hidden, d_hidden, total = (next(it) for _ in range(9))
+    page_ref, weight_ref, label_ref, feat_ref, w_one_ref, w_two_ref, one_ref, two_ref = (next(it) for _ in range(8))
+    loose, pages_all, key_s, low_s, weight_s, active, spread, hidden, d_hidden, total = (next(it) for _ in range(10))
     inner, own, owner_steps, grad_steps = plan
     all_steps = inner + own
-    chunks = own[0][1]
+    low_step, high_step = split_axis("mlp", (2, None))
+    chunks = lax.axis_size("own")
     held = [next(it) for _ in inner]
     recv = [next(it) for _ in inner]
     own_held, own_recv, full = (next(it) for _ in range(3))
@@ -386,7 +406,7 @@
     page_sems = pairs(len(owner_steps))
     inner_sems = pairs(len(inner))
     own_sems = pairs(1)[0]
-    full_sems = pairs(len(all_steps))
+    land_sems, cross_sems, core_sems = pairs(3)
     scatter_sems = pairs(len(grad_steps))
     gather_sems = pairs(len(grad_steps))
 
@@ -400,7 +420,16 @@
     started = []
 
     greet(all_steps)
-    pages_all[(0,) + tuple(place(s) for s in reversed(owner_steps))] = packed_ref[...]
+    ids = page_ref[...]
+    loose[0] = (ids // LOW).astype(jnp.float32)
+    loose[1] = (ids % LOW).astype(jnp.float32)
+    loose[2] = weight_ref[...].astype(jnp.float32)
+    count = ids.shape[0] // GROUP
+    lists = [
+        jnp.concatenate([loose[a, pl.ds(j, count, stride=GROUP), :] for j in range(GROUP)], axis=1)
+        for a in range(3)
+    ]
+    pages_all[(0,) + tuple(place(s) for s in reversed(owner_steps))] = jnp.stack(lists).astype(jnp.bfloat16)
     w_one_t = w_one_ref[...].T
     stages = len(owner_steps)
     tiles = rows_dev // 512
@@ -412,15 +441,14 @@
             active[:, i * 512 : (i + 1) * 512] = jnp.maximum(pre, 0.0).astype(jnp.bfloat16)
         settle(flying)
 
-    lists = pages_all[0]
+    lists = pages_all[0].astype(jnp.float32)
     lead = (slice(None),) * stages
-    page = lists[lead + (0,)].reshape(-1, span)
-    weight_s[...] = lists[lead + (1,)].reshape(-1, span)
-    local = page.astype(jnp.int32) - lax.axis_index(("own", "col")) * rows_dev
-    here = (local >= 0) & (local < rows_dev)
-    lane_target = lax.broadcasted_iota(jnp.int32, local.shape, 1) // width_k
-    key_s[...] = jnp.where(here, (local // LOW) * GROUP + lane_target, -1).astype(jnp.float32)
-    low_s[...] = jnp.where(here, local % LOW, -1).astype(jnp.float32)
+    local = lists[lead + (0,)].reshape(-1, span) - (lax.axis_index(("own", "col")) * high).astype(jnp.float32)
+    here = (local >= 0) & (local < high)
+    lane_target = (lax.broadcasted_iota(jnp.int32, local.shape, 1) // width_k).astype(jnp.float32)
+    key_s[...] = jnp.where(here, local * GROUP + lane_target, -1.0)
+    low_s[...] = lists[lead + (1,)].reshape(-1, span)
+    weight_s[...] = lists[lead + (2,)].reshape(-1, span)
 
     zero = jnp.zeros((), jnp.bfloat16)
     one = jnp.ones((), jnp.bfloat16)
@@ -453,7 +481,8 @@
             if k + 1 < len(inner):
                 held[k + 1][c] = part.reshape(held[k + 1].shape[1:])
             else:
-                own_held[0, 0, c] = part[0]
+                each = own[0][1] // chunks
+                own_held[0, 0, c * each : (c + 1) * each] = part
 
     running = []
     w_two_t = w_two_ref[...].T
@@ -474,10 +503,46 @@
         advance(running)
     settle(start_scatter(own[0], 0, own_held, own_recv, own_sems, started))
     logits = scatter_total(own[0], 0, own_held, own_recv)[0]
-    d_logits = softmax_gradient([logits], label_ref)[0].astype(jnp.bfloat16)
-    full[(0,) + tuple(place(s) for s in reversed(all_steps))] = d_logits
-    for k in range(len(all_steps) - 1, -1, -1):
-        settle(start_gather(all_steps, k, 0, full, full_sems[k], started))
+    rows = logits.shape[0]
+    at_label = lax.broadcasted_iota(jnp.int32, (rows, label_ref.shape[1]), 0) + lax.axis_index("mlp") * rows
+    lane = lax.broadcasted_iota(jnp.int32, at_label.shape, 1)
+    label = jnp.sum(jnp.where(lane == at_label, label_ref[...].astype(jnp.float32), 0.0), axis=1, keepdims=True)
+    exponent = jnp.exp(logits)
+    category = lax.broadcasted_iota(jnp.int32, logits.shape, 1).astype(jnp.float32)
+    probability = exponent / jnp.sum(exponent, axis=1, keepdims=True)
+    d_logits = (probability - jnp.where(category == label, 1.0, 0.0)).astype(jnp.bfloat16)
+
+    owner, upper, lower = place(own[0]), place(high_step), place(low_step)
+    full[0, owner, upper, lower] = d_logits
+
+    def send(where, sems, at, device):
+        copy = pltpu.make_async_remote_copy(
+            src_ref=full.at[where], dst_ref=full.at[where], send_sem=sems[0].at[at], recv_sem=sems[1].at[at],
+            device_id=device, device_id_type=MESH)
+        copy.start()
+        started.append(copy)
+        return copy
+
+    members = own[0][1]
+    landing = [
+        send((0, owner, upper, lower), land_sems, (shift - 1,), partner(own[0], shift)[1])
+        for shift in range(1, members)
+    ]
+    crossing = []
+    for shift in range(members):
+        if shift:
+            landing[shift - 1].wait_recv()
+        origin = lax.rem(owner + members - shift, members)
+        for hop in range(1, high_step[1]):
+            crossing.append(send(
+                (0, origin, upper, lower), cross_sems, (shift, hop - 1), partner(high_step, hop)[1]))
+    other_core = partner(low_step, 1)[1]
+    final = [send((0, slice(None), upper, lower), core_sems, (0,), other_core)]
+    settle(crossing)
+    for hop in range(1, high_step[1]):
+        origin = lax.rem(upper + high_step[1] - hop, high_step[1])
+        final.append(send((0, slice(None), origin, lower), core_sems, (hop,), other_core))
+    settle(final)
     d_logits = full[0].reshape(targets, classes)
 
     def sum_grads(p, values):
@@ -523,8 +588,7 @@
                 total[...] = product
             else:
                 total[...] += product
-            if r % 2 == 1:
-                advance(running)
+            advance(running)
         for q in range(part_units // LANES):
             launch(u * (part_units // LANES) + q, total[q * LANES : (q + 1) * LANES, :].T)
     while running:
@@ -533,21 +597,21 @@
         copy.wait_send()
 
 
-def fused(packed, labels, features, w_one, w_two, owner_steps):
-    inner = split_axis("mlp", (2, None)) + split_axis("col", (2, None))
-    own = split_axis("own", (None,))
-    grad_steps = split_axis("col", (2, None)) + split_axis("own", (2, None))
+def fused(nbr_page, nbr_weight, labels, features, w_one, w_two, owner_steps):
+    inner = split_axis("mlp", (None,))
+    own = [joined(owner_steps)]
+    grad_steps = owner_steps
     all_steps = inner + own
     rows_dev, width_f = features.shape
     units, classes = w_two.shape
-    lists, list_rows, span = packed.shape
+    lists, list_rows, span = 3, nbr_page.shape[0] // GROUP, GROUP * nbr_page.shape[1]
     sizes = lambda steps: [s[1] for s in steps]
     owners = 1
     for size in sizes(owner_steps):
         owners *= size
     groups = owners * list_rows
     targets = groups * GROUP
-    chunks = own[0][1]
+    chunks = lax.axis_size("own")
     bf16 = lambda *shape: pltpu.VMEM(shape, jnp.bfloat16)
     f32 = lambda *shape: pltpu.VMEM(shape, jnp.float32)
 
@@ -559,34 +623,36 @@
             recv.append(bf16(pieces, size - 1, outer, *block))
         return held, recv
 
-    own_rows = targets // chunks
+    own_rows = targets // owners
     for size in sizes(inner):
         own_rows //= size
+    upper = lax.axis_size("mlp") // 2
     pieces = (units + classes) // LANES
     grad_rows = width_f // owners
     held, recv = buffers(inner, chunks, targets // chunks // own_rows, own_rows, classes)
-    own_held, own_recv = buffers(own, 1, chunks, own_rows, classes)
+    own_held, own_recv = buffers(own, 1, owners, own_rows, classes)
     grad_held, grad_recv = buffers(grad_steps, pieces, owners, grad_rows, LANES)
 
     def sems(steps, count):
         return [pltpu.SemaphoreType.DMA((count, s - 1)) for s in sizes(steps) for _ in range(2)]
 
     scratch = [
-        f32(1, *reversed(sizes(owner_steps)), lists, list_rows, span),
+        f32(lists, *nbr_page.shape), bf16(1, *reversed(sizes(owner_steps)), lists, list_rows, span),
         f32(groups, span), f32(groups, span), f32(groups, span),
         bf16(units, rows_dev), bf16(targets, rows_dev), bf16(units, targets), bf16(units, targets),
         f32(256, width_f),
         *held, *recv, *own_held, *own_recv,
-        bf16(1, *reversed(sizes(all_steps)), own_rows, classes),
+        bf16(1, owners, upper, 2, own_rows, classes),
         *grad_held, *grad_recv,
         bf16(pieces, *reversed(sizes(grad_steps)), grad_rows, LANES),
-        *sems(owner_steps, 1), *sems(inner, chunks), *sems(own, 1), *sems(all_steps, 1),
+        *sems(owner_steps, 1), *sems(inner, chunks), *sems(own, 1),
+        *[pltpu.SemaphoreType.DMA(shape) for shape in ((owners - 1,), (owners, upper - 1), (upper,)) for _ in range(2)],
         *sems(grad_steps, pieces), *sems(grad_steps, pieces),
     ]
     vmem = pl.BlockSpec(memory_space=pltpu.VMEM)
     return pl.pallas_call(
         functools.partial(fused_kernel, (inner, own, owner_steps, grad_steps)),
-        in_specs=[vmem] * 5,
+        in_specs=[vmem] * 6,
         out_specs=[vmem] * 2,
         out_shape=[
             jax.ShapeDtypeStruct((width_f, units), jnp.bfloat16),
@@ -595,7 +661,7 @@
         scratch_shapes=scratch,
         compiler_params=pltpu.CompilerParams(
             collective_id=3, has_side_effects=True, vmem_limit_bytes=VMEM_LIMIT),
-    )(packed, labels, features, w_one, w_two)
+    )(nbr_page, nbr_weight, labels.reshape(1, -1), features, w_one, w_two)
 
 
 def body(features, nbr_page, nbr_weight, labels, w_one, w_two):
@@ -606,9 +672,9 @@
     owner_steps = split_axis("col", (2, None)) + split_axis("own", (None,))
     all_steps = split_axis("mlp", (2, None)) + owner_steps
     owners = lax.axis_size(own_axes)
-    if targets_dev * owners * features.shape[0] <= SPREAD_LIMIT:
-        packed = jnp.stack([nbr_page.astype(jnp.float32), nbr_weight.astype(jnp.float32)])
-        one, two = fused(packed.reshape(2, -1, span), labels[:, None], features, w_one, w_two, owner_steps)
+    small = targets_dev * owners * features.shape[0] <= SPREAD_LIMIT
+    if small and owners * features.shape[0] <= LOW * LOW and lax.axis_size("mlp") >= 4:
+        one, two = fused(nbr_page, nbr_weight, labels, features, w_one, w_two, owner_steps)
         return one.astype(jnp.float32), two.astype(jnp.float32)
     pages, weights = gather_blocks(
         (nbr_page.reshape(-1, span), nbr_weight.reshape(-1, span)), owner_steps, 0)

time: 109 us -> 112 us (1.028)
  Pallas kernels: 100 us -> 104 us
  other arithmetic: 5.26 us -> 3.92 us
    pallas_call x1, Pallas kernels: 100 us -> 104 us  [fused(): pl.pallas_call(functools.partial(fused_kernel, (inner, own, owner_steps,...]
    unnamed x0 -> x2, local copies, waits for them, and re-layouts: none -> 2.86 us
    broadcast_in_dim x1 -> x0, local copies, waits for them, and re-layouts: 1.39 us -> none  [body(): labels[:, None]]
where the time goes in v4:
time: 112 us
  Pallas kernels  104 us (93%)
  other arithmetic  3.92 us (4%)
  local copies, waits for them, and re-layouts  2.86 us (3%)
    pallas_call x1, Pallas kernels, fused(): pl.pallas_call(functools.partial(fused_kernel, (inner, own, owner_steps,...  104 us
    convert_element_type x2, other arithmetic, body(): return (one.astype(jnp.float32), two.astype(jnp.float32))  3.92 us
    unnamed x2, local copies, waits for them, and re-layouts  2.86 us

profile of v4, /device:TPU:0, one launch (start us, length us, event | category | flops | bytes accessed | tf_op | source)
XLA Modules:
  0.0 111.9 jit_solution(14633609663925710690)
XLA Ops:
  0.6 1.4 %copy.9.refs_1_ = bf16[128,32]{1,0:T(8,128)(2,1)} copy(bf16[128,32]{0,1:T(8,128)(2,1)} %param.8) | data formatting | bytes 16384 | tf_op args[2]
  2.0 1.4 %copy.8.refs_0_ = s32[128,32]{1,0:T(8,128)} copy(s32[128,32]{0,1:T(8,128)} %param.7) | data formatting | bytes 32768 | tf_op args[1]
  3.5 104.5 %shard_map.77 = (bf16[512,512]{1,0:T(8,128)(2,1)}, bf16[512,256]{1,0:T(8,128)(2,1)}) custom-call(s32[128,32]{1,0:T(8,128)} %copy.8.refs_0_, bf16[128,32]{1,0:T(8,128)(2,1)} %copy.9.refs_1_, s32[1,128]{1,0:T(1,128)} %bitcast.1, bf16[4096,512]{1,0:T(8,128)(2,1)} %refs_3_.1, bf16[512,512]{1,0:T(8,128)(2,1)} %refs_4_.1, bf16[512,256]{1,0:T(8,128)(2,1)} %refs_5_.1), custom_call_target="tpu_custom_call" | custom-call | tf_op jit(solution)/shard_map/pallas_call | solution.py:653
  108.0 2.1 %convert_element_type.6 = f32[512,512]{1,0:T(8,128)} convert(bf16[512,512]{1,0:T(8,128)(2,1)} %get-tuple-element.4) | non-fusion elementwise | flops 262144 | bytes 1572864 | tf_op jit(solution)/shard_map/convert_element_type | solution.py:678
  110.1 1.8 %convert_element_type.7 = f32[512,256]{1,0:T(8,128)} convert(bf16[512,256]{1,0:T(8,128)(2,1)} %get-tuple-element.5) | non-fusion elementwise | flops 131072 | bytes 786432 | tf_op jit(solution)/shard_map/convert_element_type | solution.py:678

commit v5 on v4

--- a/solution.py
+++ b/solution.py
@@ -391,7 +391,7 @@
 def fused_kernel(plan, *refs):
     it = iter(refs)
     page_ref, weight_ref, label_ref, feat_ref, w_one_ref, w_two_ref, one_ref, two_ref = (next(it) for _ in range(8))
-    loose, pages_all, key_s, low_s, weight_s, active, spread, hidden, d_hidden, total = (next(it) for _ in range(10))
+    loose, pages_all, key_s, low_s, weight_s, active, active_t, spread, hidden, d_hidden, total = (next(it) for _ in range(11))
     inner, own, owner_steps, grad_steps = plan
     all_steps = inner + own
     low_step, high_step = split_axis("mlp", (2, None))
@@ -421,24 +421,23 @@
 
     greet(all_steps)
     ids = page_ref[...]
-    loose[0] = (ids // LOW).astype(jnp.float32)
-    loose[1] = (ids % LOW).astype(jnp.float32)
-    loose[2] = weight_ref[...].astype(jnp.float32)
-    count = ids.shape[0] // GROUP
+    loose[0] = (ids // LOW).astype(jnp.float32).T
+    loose[1] = (ids % LOW).astype(jnp.float32).T
+    loose[2] = weight_ref[...].astype(jnp.float32).T
+    count = ids.shape[1] // GROUP
     lists = [
         jnp.concatenate([loose[a, pl.ds(j, count, stride=GROUP), :] for j in range(GROUP)], axis=1)
         for a in range(3)
     ]
     pages_all[(0,) + tuple(place(s) for s in reversed(owner_steps))] = jnp.stack(lists).astype(jnp.bfloat16)
-    w_one_t = w_one_ref[...].T
     stages = len(owner_steps)
     tiles = rows_dev // 512
     for k in range(stages - 1, -1, -1):
         flying = start_gather(owner_steps, k, 0, pages_all, page_sems[k], started)
         done = stages - 1 - k
         for i in range(done * tiles // stages, (done + 1) * tiles // stages):
-            pre = dot_nt(w_one_t, feat_ref[i * 512 : (i + 1) * 512, :])
-            active[:, i * 512 : (i + 1) * 512] = jnp.maximum(pre, 0.0).astype(jnp.bfloat16)
+            pre = dot(feat_ref[i * 512 : (i + 1) * 512, :], w_one_ref[...])
+            active[i * 512 : (i + 1) * 512, :] = jnp.maximum(pre, 0.0).astype(jnp.bfloat16)
         settle(flying)
 
     lists = pages_all[0].astype(jnp.float32)
@@ -447,25 +446,28 @@
     here = (local >= 0) & (local < high)
     lane_target = (lax.broadcasted_iota(jnp.int32, local.shape, 1) // width_k).astype(jnp.float32)
     key_s[...] = jnp.where(here, local * GROUP + lane_target, -1.0)
-    low_s[...] = lists[lead + (1,)].reshape(-1, span)
+    low = lists[lead + (1,)].reshape(-1, span)
+    for b in range(low_s.shape[0]):
+        low_s[b] = low[b * 8 : (b + 1) * 8, :].T
     weight_s[...] = lists[lead + (2,)].reshape(-1, span)
 
     zero = jnp.zeros((), jnp.bfloat16)
     one = jnp.ones((), jnp.bfloat16)
     key_rows = lax.broadcasted_iota(jnp.int32, (high * GROUP, span), 0).astype(jnp.float32).astype(jnp.bfloat16)
-    low_rows = lax.broadcasted_iota(jnp.int32, (LOW, span), 0).astype(jnp.float32).astype(jnp.bfloat16)
+    low_lanes = lax.broadcasted_iota(jnp.int32, (span, LOW), 1).astype(jnp.float32).astype(jnp.bfloat16)
 
     def build(i, carry):
         at = pl.ds(pl.multiple_of(i * 8, 8), 8)
         key = key_s[at, :].astype(jnp.bfloat16)
-        low = low_s[at, :].astype(jnp.bfloat16)
+        low = low_s[i]
         weight = weight_s[at, :].astype(jnp.bfloat16)
         for pair in range(4):
             parts = []
             for g in (2 * pair, 2 * pair + 1):
                 left = jnp.where(key_rows == key[g : g + 1, :], weight[g : g + 1, :], zero)
-                right = jnp.where(low_rows == low[g : g + 1, :], one, zero)
-                parts.append(dot_nt(left, right))
+                column = jnp.broadcast_to(low[:, g : g + 1], (span, LOW)).astype(jnp.bfloat16)
+                right = jnp.where(low_lanes == column, one, zero)
+                parts.append(dot(left, right))
             rows = pl.ds(pl.multiple_of(i * 64 + pair * 16, 16), 16)
             for h in range(high):
                 both = [p[h * GROUP : (h + 1) * GROUP, :] for p in parts]
@@ -485,7 +487,6 @@
                 own_held[0, 0, c * each : (c + 1) * each] = part
 
     running = []
-    w_two_t = w_two_ref[...].T
     blocks = chunk // 64
     for c in range(chunks):
         half = blocks // 2
@@ -493,15 +494,25 @@
         advance(running)
         lax.fori_loop(c * blocks + half, (c + 1) * blocks, build, 0)
         advance(running)
-        block = dot_nt(active[...], spread[c * chunk : (c + 1) * chunk, :]).astype(jnp.bfloat16)
-        hidden[:, c * chunk : (c + 1) * chunk] = block
-        held[0][c] = dot(w_two_t, block).T.astype(jnp.bfloat16).reshape(held[0].shape[1:])
+        block = dot(spread[c * chunk : (c + 1) * chunk, :], active[...]).astype(jnp.bfloat16)
+        hidden[c * chunk : (c + 1) * chunk, :] = block
+        held[0][c] = dot(block, w_two_ref[...]).astype(jnp.bfloat16).reshape(held[0].shape[1:])
         advance(running)
         running.append(sum_logits(c))
         next(running[-1])
+    w_one_t = w_one_ref[...].T
+
+    def transposed(first, last):
+        for i in range(first * tiles // 8, last * tiles // 8):
+            pre = dot_nt(w_one_t, feat_ref[i * 512 : (i + 1) * 512, :])
+            active_t[:, i * 512 : (i + 1) * 512] = jnp.maximum(pre, 0.0).astype(jnp.bfloat16)
+
+    transposed(0, 2)
     while running:
         advance(running)
-    settle(start_scatter(own[0], 0, own_held, own_recv, own_sems, started))
+    flying = start_scatter(own[0], 0, own_held, own_recv, own_sems, started)
+    transposed(2, 5)
+    settle(flying)
     logits = scatter_total(own[0], 0, own_held, own_recv)[0]
     rows = logits.shape[0]
     at_label = lax.broadcasted_iota(jnp.int32, (rows, label_ref.shape[1]), 0) + lax.axis_index("mlp") * rows
@@ -528,6 +539,7 @@
         send((0, owner, upper, lower), land_sems, (shift - 1,), partner(own[0], shift)[1])
         for shift in range(1, members)
     ]
+    transposed(5, 7)
     crossing = []
     for shift in range(members):
         if shift:
@@ -538,6 +550,7 @@
                 (0, origin, upper, lower), cross_sems, (shift, hop - 1), partner(high_step, hop)[1]))
     other_core = partner(low_step, 1)[1]
     final = [send((0, slice(None), upper, lower), core_sems, (0,), other_core)]
+    transposed(7, 8)
     settle(crossing)
     for hop in range(1, high_step[1]):
         origin = lax.rem(upper + high_step[1] - hop, high_step[1])
@@ -560,7 +573,7 @@
             copies = start_gather(grad_steps, k, p, grad_full, gather_sems[k], started)
             yield
             settle(copies)
-        block = grad_full[p].reshape(width_f, LANES)
+        block = grad_full[p].reshape(width_f, LANES).astype(jnp.float32)
         if p < units // LANES:
             one_ref[:, p * LANES : (p + 1) * LANES] = block
         else:
@@ -571,10 +584,11 @@
         running.append(sum_grads(p, values))
         next(running[-1])
 
-    grad_two = dot(hidden[...], d_logits)
+    d_logits_t = d_logits.T
+    grad_two = dot(d_logits_t, hidden[...]).T
     for q in range(classes // LANES):
         launch(units // LANES + q, grad_two[:, q * LANES : (q + 1) * LANES])
-    d_hidden[...] = dot_nt(w_two_ref[...], d_logits).astype(jnp.bfloat16)
+    d_hidden[...] = dot(w_two_ref[...], d_logits_t).astype(jnp.bfloat16)
     part_units = 256
     width_r = 1024
     for u in range(units // part_units):
@@ -582,7 +596,7 @@
         for r in range(rows_dev // width_r):
             at = slice(r * width_r, (r + 1) * width_r)
             spread_grad = dot(d_hidden[rows, :], spread[:, at])
-            d_pre = jnp.where(active[rows, at] > 0, spread_grad, 0.0).astype(jnp.bfloat16)
+            d_pre = jnp.where(active_t[rows, at] > 0, spread_grad, 0.0).astype(jnp.bfloat16)
             product = dot(d_pre, feat_ref[at, :])
             if r == 0:
                 total[...] = product
@@ -638,8 +652,8 @@
 
     scratch = [
         f32(lists, *nbr_page.shape), bf16(1, *reversed(sizes(owner_steps)), lists, list_rows, span),
-        f32(groups, span), f32(groups, span), f32(groups, span),
-        bf16(units, rows_dev), bf16(targets, rows_dev), bf16(units, targets), bf16(units, targets),
+        f32(groups, span), f32(groups // 8, span, 8), f32(groups, span),
+        bf16(rows_dev, units), bf16(units, rows_dev), bf16(targets, rows_dev), bf16(targets, units), bf16(units, targets),
         f32(256, width_f),
         *held, *recv, *own_held, *own_recv,
         bf16(1, owners, upper, 2, own_rows, classes),
@@ -655,13 +669,13 @@
         in_specs=[vmem] * 6,
         out_specs=[vmem] * 2,
         out_shape=[
-            jax.ShapeDtypeStruct((width_f, units), jnp.bfloat16),
-            jax.ShapeDtypeStruct((units, classes), jnp.bfloat16),
+            jax.ShapeDtypeStruct((width_f, units), jnp.float32),
+            jax.ShapeDtypeStruct((units, classes), jnp.float32),
         ],
         scratch_shapes=scratch,
         compiler_params=pltpu.CompilerParams(
             collective_id=3, has_side_effects=True, vmem_limit_bytes=VMEM_LIMIT),
-    )(nbr_page, nbr_weight, labels.reshape(1, -1), features, w_one, w_two)
+    )(nbr_page.T, nbr_weight.T, labels.reshape(1, -1), features, w_one, w_two)
 
 
 def body(features, nbr_page, nbr_weight, labels, w_one, w_two):
@@ -675,7 +689,7 @@
     small = targets_dev * owners * features.shape[0] <= SPREAD_LIMIT
     if small and owners * features.shape[0] <= LOW * LOW and lax.axis_size("mlp") >= 4:
         one, two = fused(nbr_page, nbr_weight, labels, features, w_one, w_two, owner_steps)
-        return one.astype(jnp.float32), two.astype(jnp.float32)
+        return one, two
     pages, weights = gather_blocks(
         (nbr_page.reshape(-1, span), nbr_weight.reshape(-1, span)), owner_steps, 0)
     active_t, spread, hidden_t, part = forward(own_axes, pages, weights, features, w_one.T, w_two.T)

time: 112 us -> 107 us (0.955)
  other arithmetic: 3.92 us -> 0 us
  Pallas kernels: 104 us -> 102 us
  local copies, waits for them, and re-layouts: 2.86 us -> 4.13 us
    convert_element_type x2 -> x0, other arithmetic: 3.92 us -> none  [body(): return (one.astype(jnp.float32), two.astype(jnp.float32))]
    pallas_call x1, Pallas kernels: 104 us -> 102 us  [fused(): pl.pallas_call(functools.partial(fused_kernel, (inner, own, owner_steps,...]
    unnamed x2, local copies, waits for them, and re-layouts: 2.86 us -> 4.13 us
where the time goes in v5:
time: 107 us
  Pallas kernels  102 us (95%)
  local copies, waits for them, and re-layouts  4.13 us (4%)
    pallas_call x1, Pallas kernels, fused(): pl.pallas_call(functools.partial(fused_kernel, (inner, own, owner_steps,...  102 us
    unnamed x2, local copies, waits for them, and re-layouts  4.13 us

profile of v5, /device:TPU:0, one launch (start us, length us, event | category | flops | bytes accessed | tf_op | source)
XLA Modules:
  0.0 107.1 jit_solution(7490591532794740835)
XLA Ops:
  0.6 102.3 %shard_map.77 = (f32[512,512]{1,0:T(8,128)}, f32[512,256]{1,0:T(8,128)}) custom-call(s32[32,128]{1,0:T(8,128)} %bitcast.3, bf16[32,128]{1,0:T(8,128)(2,1)} %bitcast.4, s32[1,128]{1,0:T(1,128)} %bitcast.5, bf16[4096,512]{1,0:T(8,128)(2,1)} %refs_3_.1, bf16[512,512]{1,0:T(8,128)(2,1)} %refs_4_.1, bf16[512,256]{1,0:T(8,128)(2,1)} %refs_5_.1), custom_call_target="tpu_custom_call" | custom-call | tf_op jit(solution)/shard_map/pallas_call | solution.py:667
  103.0 2.3 %copy.10 = f32[512,512]{1,0:T(8,128)} copy(f32[512,512]{1,0:T(8,128)} %get-tuple-element.4) | data formatting | bytes 2097152
  105.2 1.9 %copy.11 = f32[512,256]{1,0:T(8,128)} copy(f32[512,256]{1,0:T(8,128)} %get-tuple-element.5) | data formatting | bytes 1048576

commit v6 on v5

--- a/solution.py
+++ b/solution.py
@@ -390,7 +390,8 @@
 
 def fused_kernel(plan, *refs):
     it = iter(refs)
-    page_ref, weight_ref, label_ref, feat_ref, w_one_ref, w_two_ref, one_ref, two_ref = (next(it) for _ in range(8))
+    page_ref, weight_ref, label_ref, feat_hbm, w_one_ref, w_two_ref, one_ref, two_ref = (next(it) for _ in range(8))
+    feat_ref, feat_sem = next(it), next(it)
     loose, pages_all, key_s, low_s, weight_s, active, active_t, spread, hidden, d_hidden, total = (next(it) for _ in range(11))
     inner, own, owner_steps, grad_steps = plan
     all_steps = inner + own
@@ -419,6 +420,8 @@
     high = rows_dev // LOW
     started = []
 
+    load = pltpu.make_async_copy(feat_hbm, feat_ref, feat_sem)
+    load.start()
     greet(all_steps)
     ids = page_ref[...]
     loose[0] = (ids // LOW).astype(jnp.float32).T
@@ -435,6 +438,8 @@
     for k in range(stages - 1, -1, -1):
         flying = start_gather(owner_steps, k, 0, pages_all, page_sems[k], started)
         done = stages - 1 - k
+        if done == 0:
+            load.wait()
         for i in range(done * tiles // stages, (done + 1) * tiles // stages):
             pre = dot(feat_ref[i * 512 : (i + 1) * 512, :], w_one_ref[...])
             active[i * 512 : (i + 1) * 512, :] = jnp.maximum(pre, 0.0).astype(jnp.bfloat16)
@@ -573,7 +578,7 @@
             copies = start_gather(grad_steps, k, p, grad_full, gather_sems[k], started)
             yield
             settle(copies)
-        block = grad_full[p].reshape(width_f, LANES).astype(jnp.float32)
+        block = grad_full[p].reshape(width_f, LANES)
         if p < units // LANES:
             one_ref[:, p * LANES : (p + 1) * LANES] = block
         else:
@@ -602,7 +607,8 @@
                 total[...] = product
             else:
                 total[...] += product
-            advance(running)
+            if r % 2 == 1:
+                advance(running)
         for q in range(part_units // LANES):
             launch(u * (part_units // LANES) + q, total[q * LANES : (q + 1) * LANES, :].T)
     while running:
@@ -651,7 +657,7 @@
         return [pltpu.SemaphoreType.DMA((count, s - 1)) for s in sizes(steps) for _ in range(2)]
 
     scratch = [
-        f32(lists, *nbr_page.shape), bf16(1, *reversed(sizes(owner_steps)), lists, list_rows, span),
+        bf16(rows_dev, width_f), pltpu.SemaphoreType.DMA, f32(lists, *nbr_page.shape), bf16(1, *reversed(sizes(owner_steps)), lists, list_rows, span),
         f32(groups, span), f32(groups // 8, span, 8), f32(groups, span),
         bf16(rows_dev, units), bf16(units, rows_dev), bf16(targets, rows_dev), bf16(targets, units), bf16(units, targets),
         f32(256, width_f),
@@ -666,16 +672,32 @@
     vmem = pl.BlockSpec(memory_space=pltpu.VMEM)
     return pl.pallas_call(
         functools.partial(fused_kernel, (inner, own, owner_steps, grad_steps)),
-        in_specs=[vmem] * 6,
+        in_specs=[vmem] * 3 + [pl.BlockSpec(memory_space=pl.ANY)] + [vmem] * 2,
         out_specs=[vmem] * 2,
         out_shape=[
-            jax.ShapeDtypeStruct((width_f, units), jnp.float32),
-            jax.ShapeDtypeStruct((units, classes), jnp.float32),
+            jax.ShapeDtypeStruct((width_f, units), jnp.bfloat16),
+            jax.ShapeDtypeStruct((units, classes), jnp.bfloat16),
         ],
         scratch_shapes=scratch,
         compiler_params=pltpu.CompilerParams(
             collective_id=3, has_side_effects=True, vmem_limit_bytes=VMEM_LIMIT),
     )(nbr_page.T, nbr_weight.T, labels.reshape(1, -1), features, w_one, w_two)
+
+
+def widen_kernel(one_ref, two_ref, one_out, two_out):
+    one_out[...] = one_ref[...].astype(jnp.float32)
+    two_out[...] = two_ref[...].astype(jnp.float32)
+
+
+def widen(one, two):
+    vmem = pl.BlockSpec(memory_space=pltpu.VMEM)
+    return pl.pallas_call(
+        widen_kernel,
+        in_specs=[vmem] * 2,
+        out_specs=[vmem] * 2,
+        out_shape=[jax.ShapeDtypeStruct(a.shape, jnp.float32) for a in (one, two)],
+        compiler_params=pltpu.CompilerParams(vmem_limit_bytes=VMEM_LIMIT),
+    )(one, two)
 
 
 def body(features, nbr_page, nbr_weight, labels, w_one, w_two):
@@ -689,7 +711,7 @@
     small = targets_dev * owners * features.shape[0] <= SPREAD_LIMIT
     if small and owners * features.shape[0] <= LOW * LOW and lax.axis_size("mlp") >= 4:
         one, two = fused(nbr_page, nbr_weight, labels, features, w_one, w_two, owner_steps)
-        return one, two
+        return widen(one, two)
     pages, weights = gather_blocks(
         (nbr_page.reshape(-1, span), nbr_weight.reshape(-1, span)), owner_steps, 0)
     active_t, spread, hidden_t, part = forward(own_axes, pages, weights, features, w_one.T, w_two.T)

time: 107 us -> 91.4 us (0.85)
  Pallas kernels: 102 us -> 90.6 us
  local copies, waits for them, and re-layouts: 4.13 us -> 0 us
    pallas_call x1, Pallas kernels: 102 us -> 88.3 us  [fused(): pl.pallas_call(functools.partial(fused_kernel, (inner, own, owner_steps,...]
    unnamed x2 -> x0, local copies, waits for them, and re-layouts: 4.13 us -> none
    pallas_call x0 -> x1, Pallas kernels: none -> 2.32 us  [widen(): pl.pallas_call(widen_kernel, in_specs=[vmem] * 2, out_specs=[vmem] * 2, o...]
where the time goes in v6:
time: 91.4 us; the launch traced here: 91.2 us
  Pallas kernels  90.6 us (99%)
    pallas_call x1, Pallas kernels, fused(): pl.pallas_call(functools.partial(fused_kernel, (inner, own, owner_steps,...  88.3 us
    pallas_call x1, Pallas kernels, widen(): pl.pallas_call(widen_kernel, in_specs=[vmem] * 2, out_specs=[vmem] * 2, o...  2.32 us

profile of v6, /device:TPU:0, one launch (start us, length us, event | category | flops | bytes accessed | tf_op | source)
XLA Modules:
  0.0 91.2 jit_solution(405697538263112957)
XLA Ops:
  0.6 88.3 %shard_map.77 = (bf16[512,512]{1,0:T(8,128)(2,1)}, bf16[512,256]{1,0:T(8,128)(2,1)}) custom-call(s32[32,128]{1,0:T(8,128)} %bitcast.3, bf16[32,128]{1,0:T(8,128)(2,1)} %bitcast.4, s32[1,128]{1,0:T(1,128)} %bitcast.5, bf16[4096,512]{1,0:T(8,128)(2,1)} %refs_3_.1, bf16[512,512]{1,0:T(8,128)(2,1)} %refs_4_.1, bf16[512,256]{1,0:T(8,128)(2,1)} %refs_5_.1), custom_call_target="tpu_custom_call" | custom-call | tf_op jit(solution)/shard_map/pallas_call | solution.py:673
  88.9 2.3 %shard_map.78 = (f32[512,512]{1,0:T(8,128)}, f32[512,256]{1,0:T(8,128)}) custom-call(bf16[512,512]{1,0:T(8,128)(2,1)} %get-tuple-element.4.one_ref, bf16[512,256]{1,0:T(8,128)(2,1)} %get-tuple-element.5.two_ref), custom_call_target="tpu_custom_call" | custom-call | tf_op jit(solution)/shard_map/pallas_call | solution.py:694
